TPU v7x, 32 devices: a whole 2x2x4 slice. The times are simulated.
32 devices in a mesh: ctx: 8 (over z, x), fsdp: 4 (over y, core).
Axes of the slice: x: 2, y: 2, z: 4, core: 2. Of those that a mesh axis runs over, the one named last changes fastest.
Arguments:
- layer_in: bfloat16 [4, 1024, 4096], P('fsdp', 'ctx'), may hold values from -6 to 6
- w_bc: bfloat16 [4096, 256], P('fsdp'), may hold values from -0.09375 to 0.09375
- conv_w: float32 [4, 256], replicated, may hold values from -3 to 3
- conv_b: float32 [256], replicated, may hold values from -0.5 to 0.5
- ssm_in: bfloat16 [4, 1024, 4096], P('fsdp', 'ctx'), may hold values from -6 to 6
- dt_raw: float32 [4, 1024, 32], P('fsdp', 'ctx'), may hold values from -4 to 4
- dt_bias: float32 [32], replicated, as said below
- a_log: float32 [32], replicated, as said below
- skip_scale: float32 [32], replicated, may hold values from 0.5 to 1.5
- grad_out: bfloat16 [4, 1024, 4096], P('fsdp', 'ctx'), may hold values from -6 to 6
Outputs:
- ssm_out: bfloat16 [4, 1024, 4096], P('fsdp', 'ctx')
- grad_ssm_in: bfloat16 [4, 1024, 4096], P('fsdp', 'ctx')
- grad_layer_in: bfloat16 [4, 1024, 4096], P('fsdp', 'ctx')
- grad_dt_raw: float32 [4, 1024, 32], P('fsdp', 'ctx')
- grad_w_bc: float32 [4096, 256], P('fsdp')
- grad_conv_w: float32 [4, 256], replicated
- grad_conv_b: float32 [256], replicated
- grad_dt_bias: float32 [32], replicated
- grad_a_log: float32 [32], replicated
- grad_skip: float32 [32], replicated
Inputs may be any that keep to these rules, and one draw needn't show every extreme that they name: `dt_bias`: drawn together with a_log. `a_log`: drawn together with dt_bias.
All inputs are finite; a program needn't handle non-finite values.
Results may differ from a plain program's by a relative error of at most 0.039.
Values may be sent and summed in bfloat16 or wider, within the bound.
No kernel may reach another device: no remote copies, remote signals or barrier semaphores. Data moves between devices by JAX's collectives and lax.ppermute only.
A program may use at most 320 MiB of HBM per device.

v0:
```python
import jax
import jax.numpy as jnp
from jax import lax
from jax.sharding import PartitionSpec as P

SPAN = 128


def carried_in(x, axis, join, neutral):
    place = lax.axis_index(axis)
    gathered = jax.tree.map(
        lambda a, kind: lax.all_gather(a.astype(kind), axis), x, (jnp.bfloat16, jnp.bfloat16)
    )
    state = jax.tree.map(lambda a, e: jnp.zeros_like(a) + jnp.asarray(e, a.dtype), x, neutral)

    def one(turn, state):
        return join(
            state,
            jax.tree.map(
                lambda a, own: lax.dynamic_index_in_dim(a, turn, 0, False).astype(own.dtype),
                gathered,
                x,
            ),
        )

    return lax.fori_loop(0, place, one, state)


def prefix(x, axis, combine, identity):
    size, here = (lax.axis_size(axis), lax.axis_index(axis))
    everything = jax.tree.map(
        lambda part, kind: lax.all_gather(part.astype(kind), axis),
        x,
        jax.tree.map(lambda a: jnp.bfloat16 if a.dtype == jnp.float32 else a.dtype, x),
    )
    start = jax.tree.map(
        lambda part, zero: jnp.broadcast_to(jnp.asarray(zero, part.dtype), part.shape), x, identity
    )

    def turn(k, before):
        at = size - 1 - k
        reached = at > here
        new = combine(
            before, jax.tree.map(lambda part, own: part[at].astype(own.dtype), everything, x)
        )
        return jax.tree.map(lambda a, b: jnp.where(reached, a, b), new, before)

    return lax.fori_loop(0, size, turn, start)


def shifted(x, axis, by):
    size = lax.axis_size(axis)
    pairs = [(i, i + by) for i in range(size) if 0 <= i + by < size]
    return lax.ppermute(x, axis, pairs)


def prepare(padded, conv_w, conv_b, dt_raw, dt_bias, a_log):
    row_count = dt_raw.shape[0]
    conv_width = conv_w.shape[0]
    conv_sum = conv_b[None, :] + conv_w[0][None, :] * padded[0:row_count]
    for offset in range(1, conv_width):
        conv_sum = conv_sum + conv_w[offset][None, :] * padded[offset : offset + row_count]
    activated = jax.nn.silu(conv_sum)
    half_width = activated.shape[1] // 2
    b_in = activated[:, :half_width].astype(jnp.bfloat16)
    c_out = activated[:, half_width:].astype(jnp.bfloat16)
    step_size = jax.nn.softplus(dt_raw + dt_bias[None, :])
    log_decay = -step_size * jnp.exp(a_log)[None, :]
    return (b_in, c_out, step_size, log_decay)


def span_local(b_in, c_out, step_size, log_decay, values, skip_scale):
    span_len = step_size.shape[0]
    cumulated = jnp.cumsum(log_decay, axis=0)
    scores = jnp.dot(c_out, b_in.T, preferred_element_type=jnp.float32)
    per_head = cumulated.T
    gap_log = per_head[:, :, None] - per_head[:, None, :]
    row_ids = lax.broadcasted_iota(jnp.int32, (span_len, span_len), 0)
    col_ids = lax.broadcasted_iota(jnp.int32, (span_len, span_len), 1)
    causal_mask = (row_ids >= col_ids)[None, :, :]
    decay_grid = jnp.where(causal_mask, jnp.exp(jnp.where(causal_mask, gap_log, 0.0)), 0.0)
    mixing = (scores[None, :, :] * decay_grid * step_size.T[:, None, :]).astype(jnp.bfloat16)
    inside_out = jnp.einsum("hij,jhp->ihp", mixing, values, preferred_element_type=jnp.float32)
    local_out = inside_out + skip_scale[None, :, None] * values.astype(jnp.float32)
    end_weight = jnp.exp(per_head[:, -1:] - per_head) * step_size.T
    deposit = (end_weight[:, :, None] * b_in.astype(jnp.float32)[None, :, :]).astype(jnp.bfloat16)
    span_state = jnp.einsum("hjn,jhp->hnp", deposit, values, preferred_element_type=jnp.float32)
    return (local_out, span_state, jnp.exp(per_head[:, -1]), jnp.exp(cumulated))


def span_output(local_out, growth, c_out, state):
    stored = state.astype(jnp.bfloat16)
    carried_out = jnp.einsum("in,hnp->ihp", c_out, stored, preferred_element_type=jnp.float32)
    return local_out + growth[:, :, None] * carried_out


def summary(padded, conv_w, conv_b, raw_steps, dt_bias, a_log, values_in, skip_scale):
    b_in, c_out, step_size, log_decay = prepare(padded, conv_w, conv_b, raw_steps, dt_bias, a_log)
    row_count = step_size.shape[0]
    head_count = step_size.shape[1]
    head_size = values_in.shape[1] // head_count
    state_size = b_in.shape[1]
    values = values_in.reshape(row_count, head_count, head_size)
    running_state = jnp.zeros((head_count, state_size, head_size), jnp.float32)
    decay_total = jnp.ones((head_count,), jnp.float32)
    local_list, growth_list, prefix_list, decay_list = ([], [], [], [])
    local_out, span_state, span_decay, growth = span_local(
        b_in, c_out, step_size, log_decay, values, skip_scale
    )
    local_list.append(local_out)
    growth_list.append(growth)
    prefix_list.append(running_state)
    decay_list.append(decay_total)
    running_state = span_decay[:, None, None] * running_state + span_state
    decay_total = decay_total * span_decay
    return (
        running_state,
        decay_total,
        jnp.stack(local_list),
        jnp.stack(growth_list),
        c_out,
        jnp.stack(prefix_list),
        jnp.stack(decay_list),
    )


def finish(entering, local_outs, growths, c_out, prefixes, decays):
    pieces = []
    for span_index in range(local_outs.shape[0]):
        first = span_index * SPAN
        state = decays[span_index][:, None, None] * entering + prefixes[span_index]
        result = span_output(
            local_outs[span_index], growths[span_index], c_out[first : first + SPAN], state
        )
        pieces.append(result.astype(jnp.bfloat16).reshape(SPAN, -1))
    return jnp.concatenate(pieces, 0)


def chain(early, late):
    return (early[0] * late[0], late[0] * early[1] + late[1])


def forward_states(decay_col, flat_state):
    identity = (jnp.ones(decay_col.shape, jnp.float32), jnp.zeros(flat_state.shape, jnp.float32))
    return carried_in((decay_col, flat_state), "ctx", chain, identity)[1]


def backward_states(decay_col, flat_grad):
    identity = (jnp.ones(decay_col.shape, jnp.float32), jnp.zeros(flat_grad.shape, jnp.float32))
    return prefix((decay_col, flat_grad), "ctx", chain, identity)[1]


def body(layer_in, w_bc, conv_w, conv_b, ssm_in, dt_raw, dt_bias, a_log, skip_scale, grad_out):
    tokens_in = layer_in[0]
    values_in = ssm_in[0]
    raw_steps = dt_raw[0]
    upstream = grad_out[0]
    row_count = tokens_in.shape[0]
    conv_width = conv_w.shape[0]
    head_count = dt_bias.shape[0]
    columns = tokens_in
    projected = jnp.dot(
        columns,
        lax.all_gather(w_bc, "fsdp", axis=0, tiled=True),
        preferred_element_type=jnp.float32,
    )
    tail_start = row_count - conv_width + 1
    rim_rows = shifted(projected[tail_start:], "ctx", 1)
    padded = jnp.concatenate([rim_rows, projected], 0)
    summary_out, summary_back = jax.vjp(
        summary, padded, conv_w, conv_b, raw_steps, dt_bias, a_log, values_in, skip_scale
    )
    device_state = summary_out[0]
    state_shape = device_state.shape
    decay_col = summary_out[1][:, None]
    entering = forward_states(decay_col, device_state.reshape(head_count, -1))
    ssm_out, finish_back = jax.vjp(finish, entering.reshape(state_shape), *summary_out[2:])
    grads_late = finish_back(upstream)
    later_grad = backward_states(decay_col, grads_late[0].reshape(head_count, -1))
    decay_grad = jnp.sum(later_grad * entering, axis=1)
    grads_early = summary_back(
        (later_grad.reshape(state_shape), decay_grad) + tuple(grads_late[1:])
    )
    grad_padded, grad_cw, grad_cb, grad_raw, grad_bias, grad_log, grad_values, grad_skip_local = (
        grads_early
    )
    rim_grad = shifted(grad_padded[: conv_width - 1], "ctx", -1)
    grad_proj = grad_padded[conv_width - 1 :]
    grad_proj = jnp.concatenate([grad_proj[:tail_start], grad_proj[tail_start:] + rim_grad], 0)
    grad_rounded = grad_proj.astype(jnp.bfloat16)
    product = lax.dot_general(
        grad_rounded,
        lax.all_gather(w_bc, "fsdp", axis=0, tiled=True),
        (((1,), (1,)), ((), ())),
        preferred_element_type=jnp.float32,
    )
    grad_tokens = product.astype(jnp.bfloat16)
    columns = tokens_in
    weight_part = lax.psum_scatter(
        lax.dot_general(
            columns, grad_rounded, (((0,), (0,)), ((), ())), preferred_element_type=jnp.float32
        ).astype(jnp.bfloat16),
        "fsdp",
        scatter_dimension=0,
        tiled=True,
    )
    grad_weight = lax.psum(weight_part, "ctx").astype(jnp.float32)
    sums = lax.psum((grad_cw, grad_cb, grad_bias, grad_log, grad_skip_local), ("ctx", "fsdp"))
    return (
        ssm_out[None],
        grad_values[None],
        grad_tokens[None],
        grad_raw[None],
        grad_weight,
        sums[0],
        sums[1],
        sums[2],
        sums[3],
        sums[4],
    )


def solution(mesh):
    in_specs = (
        P("fsdp", "ctx", None),
        P("fsdp", None),
        P(),
        P(),
        P("fsdp", "ctx", None),
        P("fsdp", "ctx", None),
        P(),
        P(),
        P(),
        P("fsdp", "ctx", None),
    )
    out_specs = (
        P("fsdp", "ctx", None),
        P("fsdp", "ctx", None),
        P("fsdp", "ctx", None),
        P("fsdp", "ctx", None),
        P("fsdp", None),
        P(),
        P(),
        P(),
        P(),
        P(),
    )
    return jax.shard_map(body, mesh=mesh, in_specs=in_specs, out_specs=out_specs, check_vma=False)
```

profile of v0, /device:TPU:0, one launch (start us, length us, event | category | flops | bytes accessed | tf_op | source)
XLA Modules:
  0.0 458.9 jit_solution(16645782837861138514)
XLA Ops:
  10.1 24.8 %all-gather.5.cloned.1.call-done = bf16[4096,256]{1,0:T(8,128)(2,1)} async-done(((bf16[1024,256]{1,0:T(8,128)(2,1)}), bf16[4096,256]{1,0:T(8,128)(2,1)}) %all-gather.5.cloned.1.call-update) | async-done | bytes 2097168 | tf_op jit(solution)/shard_map/all_gather | solution.py:164
  37.0 3.4 collective-permute-start
  47.9 22.6 %all-reduce.12 = bf16[256]{0:T(256)(128)(2,1)S(1)} all-reduce(bf16[256]{0:T(256)(128)(2,1)S(1)} %dynamic-update-slice), channel_id=2, replica_groups=mesh['ctx'=8,'fsdp'=4] {'ctx'}, use_global_device_ids=true, to_apply=%add.12 | all-reduce | flops 256 | bytes 1024
  74.9 2.9 copy.172
  84.8 3.0 add_convert_fusion
  91.0 4.2 fusion.24
  95.2 77.0 %all-gather.9.cloned.1.call-done = bf16[8,32,16384]{2,1,0:T(8,128)(2,1)} async-done(((bf16[1,32,16384]{2,1,0:T(8,128)(2,1)}), bf16[8,32,16384]{2,1,0:T(8,128)(2,1)}) %all-gather.9.cloned.1.call-update) | async-done | bytes 8388624 | tf_op jit(solution)/shard_map/all_gather | solution.py:32
  172.2 28.0 %while.29 = (s32[]{:T(128)}, f32[32,16384]{1,0:T(8,128)S(1)}, s32[]{:T(128)}, bf16[8,32,1]{1,2,0:T(2,128)(2,1)}, bf16[8,32,16384]{2,1,0:T(8,128)(2,1)}, /*index=5*/s32[]{:T(128)}, s32[]{:T(128)}, s32[]{:T(128)}, s32[]{:T(128)}) while((s32[]{:T(128)}, f32[32,16384]{1,0:T(8,128)S(1)}, s32[]{:T(128)}, bf16[8,32,1]{1,2,0:T(2,128)(2,1)}, ...), condition=%wide.region_4.5_spmd.clone, body=%wide.region_3.4_spmd.clone.sunk | while | flops 2621480 | bytes 5243375 | solution.py:48
  173.3 2.3 fusion.94
  176.8 2.3 fusion.94
  180.3 2.4 fusion.94
  183.9 2.3 fusion.94
  187.4 2.3 fusion.94
  190.9 2.3 fusion.94
  194.4 2.3 fusion.94
  197.9 2.3 fusion.94
  200.2 97.2 %all-gather.7.cloned.1.call-done = bf16[8,32,16384]{2,1,0:T(8,128)(2,1)} async-done(((bf16[1,32,16384]{2,1,0:T(8,128)(2,1)}), bf16[8,32,16384]{2,1,0:T(8,128)(2,1)}) %all-gather.7.cloned.1.call-update) | async-done | bytes 8388624 | tf_op jit(solution)/shard_map/all_gather | solution.py:12
  298.9 3.2 multiply_reduce_fusion
  311.2 6.8 %collective-permute-done.1 = f32[3,256]{1,0:T(4,128)S(1)} collective-permute-done((f32[3,256]{1,0:T(4,128)S(1)}, f32[3,256]{1,0:T(4,128)S(1)}, u32[]{:S(2)}, u32[]{:S(2)}) %collective-permute-start.1) | collective-permute-done | bytes 3104 | tf_op jit(solution)/shard_map/ppermute | solution.py:54
  327.2 2.4 copy.184
  332.3 2.4 copy.185
  337.5 36.5 %reduce-scatter.2.cloned.1.call-done = bf16[1024,256]{0,1:T(8,128)(2,1)} async-done(((bf16[4096,256]{0,1:T(8,128)(2,1)}), bf16[1024,256]{0,1:T(8,128)(2,1)}) %reduce-scatter.2.cloned.1.call-update) | async-done | bytes 524304 | tf_op jit(solution)/shard_map/reduce_scatter | solution.py:199
  374.1 39.8 %all-reduce.13 = (f32[4,256]{1,0:T(4,128)}, f32[256]{0:T(256)}, f32[32]{0:T(128)}, f32[32]{0:T(128)}, f32[32]{0:T(128)}) all-reduce(f32[4,256]{1,0:T(4,128)S(1)} %pad_add_fusion.2, f32[256]{0:T(256)S(1)} %copy-done.40, f32[32]{0:T(128)S(1)} %get-tuple-element.354, ...), channel_id=1, replica_groups=mesh['ctx'=8,'fsdp'=4] {'ctx','fsdp'}, use_global_device_ids=true, to_apply=%region_22.23 | all-reduce | flops 1376 | bytes 11008 | tf_op jit(solution)/shard_map/psum | solution.py:208
  415.7 34.5 %all-reduce.16.cloned.1.call-done = bf16[1024,256]{0,1:T(8,128)(2,1)} async-done(((bf16[1024,256]{0,1:T(8,128)(2,1)}), bf16[1024,256]{0,1:T(8,128)(2,1)}) %all-reduce.16.cloned.1.call-update) | async-done | bytes 524304 | tf_op jit(solution)/shard_map/psum | solution.py:207
  (197 shorter events, 64.4 us)
Async XLA Ops:
  7.2 27.8 %copy-start = (bf16[1,128,4096]{2,1,0:T(8,128)(2,1)S(1)}, bf16[1,128,4096]{2,1,0:T(8,128)(2,1)}, u32[]{:S(2)}) copy-start(bf16[1,128,4096]{2,1,0:T(8,128)(2,1)} %param.14) | copy-start | bytes 3145732
  7.2 33.2 %copy-start.45 = (f32[4,256]{1,0:T(4,128)S(1)}, f32[4,256]{1,0:T(4,128)}, u32[]{:S(2)}) copy-start(f32[4,256]{1,0:T(4,128)} %param.16) | copy-start | bytes 12292
  7.2 33.2 %copy-start.3 = (bf16[1,128,4096]{2,1,0:T(8,128)(2,1)S(1)}, bf16[1,128,4096]{2,1,0:T(8,128)(2,1)}, u32[]{:S(2)}) copy-start(bf16[1,128,4096]{2,1,0:T(8,128)(2,1)} %param.23) | copy-start | bytes 3145732
  7.2 27.7 %all-gather.5.cloned.1.call-start = ((), (), s32[]{:S(2)}) async-start(), calls=%async_computation.1 | async-start | bytes 2621440 | tf_op jit(solution)/shard_map/all_gather | solution.py:164
  7.9 164.2 %all-gather.9.cloned.1.call-start = ((), (), s32[]{:S(2)}) async-start(), calls=%async_computation.3 | async-start | bytes 9437184 | tf_op jit(solution)/shard_map/all_gather | solution.py:32
  8.7 32.5 %copy-start.46 = (f32[32]{0:T(128)}, f32[32]{0:T(128)S(1)}, u32[]{:S(2)}) copy-start(f32[32]{0:T(128)S(1)} %exp.44) | copy-start | bytes 388
  10.1 31.6 %copy-start.48 = (f32[256]{0:T(256)S(1)}, f32[256]{0:T(256)}, u32[]{:S(2)}) copy-start(f32[256]{0:T(256)} %param.17) | copy-start | bytes 3076
  37.0 4.7 %collective-permute-start = (f32[3,256]{1,0:T(4,128)S(1)}, f32[3,256]{1,0:T(4,128)S(1)}, u32[]{:S(2)}, u32[]{:S(2)}) collective-permute-start(f32[3,256]{1,0:T(4,128)S(1)} %slice.63), channel_id=1, source_target_pairs={{0,4},{4,8},{8,12},{12,16},{16,20},{20,24},{24,28},{1,5},{5,9},{9,... | collective-permute-start | bytes 9224 | tf_op jit(solution)/shard_map/ppermute | solution.py:54
  41.5 32.0 %copy-start.14 = (f32[128,32]{0,1:T(8,128)}, f32[128,32]{0,1:T(8,128)S(1)}, u32[]{:S(2)}) copy-start(f32[128,32]{0,1:T(8,128)S(1)} %exp.46) | copy-start | bytes 49156
  46.2 251.3 %all-gather.7.cloned.1.call-start = ((), (), s32[]{:S(2)}) async-start(), calls=%async_computation.2 | async-start | bytes 9437184 | tf_op jit(solution)/shard_map/all_gather | solution.py:12
  90.9 283.0 %reduce-scatter.2.cloned.1.call-start = ((), (), s32[]{:S(2)}) async-start(), calls=%async_computation.4 | async-start | bytes 2621440 | tf_op jit(solution)/shard_map/reduce_scatter | solution.py:199
  303.7 4.6 %copy-start.8 = (bf16[4,8,128,128]{3,2,1,0:T(8,128)(2,1)S(1)}, bf16[4,8,128,128]{3,2,1,0:T(8,128)(2,1)}, u32[]{:S(2)}) copy-start(bf16[4,8,128,128]{3,2,1,0:T(8,128)(2,1)} %copy.193) | copy-start | bytes 3145732
  303.8 4.6 %copy-start.11 = (bf16[16,8,32,128]{3,2,1,0:T(8,128)(2,1)S(1)}, bf16[16,8,32,128]{3,2,1,0:T(8,128)(2,1)}, u32[]{:S(2)}) copy-start(bf16[16,8,32,128]{3,2,1,0:T(8,128)(2,1)} %copy.195) | copy-start | bytes 3145732
  309.8 8.2 %collective-permute-start.1 = (f32[3,256]{1,0:T(4,128)S(1)}, f32[3,256]{1,0:T(4,128)S(1)}, u32[]{:S(2)}, u32[]{:S(2)}) collective-permute-start(f32[3,256]{1,0:T(4,128)S(1)} %pad_add_fusion.1), channel_id=1, source_target_pairs={{4,0},{8,4},{12,8},{16,12},{20,16},{24,20},{28,24},{5,1},{9,5},{13... | collective-permute-start | bytes 9224 | tf_op jit(solution)/shard_map/ppermute | solution.py:54
  320.1 130.0 %all-reduce.16.cloned.1.call-start = ((), (), s32[]{:S(2)}) async-start(), calls=%async_computation.5 | async-start | bytes 1048576 | tf_op jit(solution)/shard_map/psum | solution.py:207
  330.2 4.6 copy-start.13
  330.2 4.6 copy-start.20
  332.3 41.7 %copy-start.41 = (f32[256]{0:T(256)S(1)}, f32[256]{0:T(256)}, u32[]{:S(2)}) copy-start(f32[256]{0:T(256)} %get-tuple-element.324) | copy-start | bytes 3076
  332.3 41.7 %copy-start.42 = (f32[256]{0:T(256)S(1)}, f32[256]{0:T(256)}, u32[]{:S(2)}) copy-start(f32[256]{0:T(256)} %get-tuple-element.325) | copy-start | bytes 3076
  332.3 41.7 %copy-start.43 = (f32[256]{0:T(256)S(1)}, f32[256]{0:T(256)}, u32[]{:S(2)}) copy-start(f32[256]{0:T(256)} %get-tuple-element.326) | copy-start | bytes 3076
  332.3 41.7 %copy-start.44 = (f32[256]{0:T(256)S(1)}, f32[256]{0:T(256)}, u32[]{:S(2)}) copy-start(f32[256]{0:T(256)} %get-tuple-element.327) | copy-start | bytes 3076
  332.3 41.7 %copy-start.52 = (f32[32]{0:T(128)S(1)}, f32[32]{0:T(128)}, u32[]{:S(2)}) copy-start(f32[32]{0:T(128)} %param.21) | copy-start | bytes 388
  332.3 41.7 %copy-start.40 = (f32[256]{0:T(256)S(1)}, f32[256]{0:T(256)}, u32[]{:S(2)}) copy-start(f32[256]{0:T(256)} %get-tuple-element.328) | copy-start | bytes 3076
  332.3 81.5 %copy-start.5 = (bf16[4096,256]{1,0:T(8,128)(2,1)S(1)}, bf16[4096,256]{1,0:T(8,128)(2,1)}, u32[]{:S(2)}) copy-start(bf16[4096,256]{1,0:T(8,128)(2,1)} %all-gather.5.cloned.1.call-done) | copy-start | bytes 6291460
  (37 other events, 89.9 us)
Sparse Core Ops, SparseCore 0:
  9.6 25.2 all-gather.4
  46.3 125.8 all-gather.8
  174.3 123.1 all-gather.6
  320.2 53.6 reduce-scatter.1
  377.6 72.5 all-reduce.15
where the time goes:
time: 460 us; the launch traced here: 459 us
  waiting for transfers between devices  278 us (60%)
  blocking collectives  62.4 us (14%)
  other arithmetic  42.4 us (9%)
  local copies, waits for them, and re-layouts  32.6 us (7%)
  matrix products  23.3 us (5%)
  between operations  15.2 us (3%)
  starting transfers between devices  5.05 us (1%)
    all_gather x1, waiting for transfers between devices, carried_in(): lax.all_gather(a.astype(kind), axis)  97.2 us
    all_gather x1, waiting for transfers between devices, prefix(): lax.all_gather(part.astype(kind), axis)  77 us
    psum x1, blocking collectives, body(): lax.psum((grad_cw, grad_cb, grad_bias, grad_log, grad_skip_local), ('ctx'...  39.8 us
    reduce_scatter x1, waiting for transfers between devices, body(): lax.psum_scatter(lax.dot_general(columns, grad_rounded, (((0,), (0,)), ((...  36.5 us
    psum x1, waiting for transfers between devices, body(): grad_weight = lax.psum(weight_part, 'ctx').astype(jnp.float32)  34.5 us
    all_gather x1, waiting for transfers between devices, body(): lax.all_gather(w_bc, 'fsdp', axis=0, tiled=True)  24.8 us
    unnamed x1, blocking collectives  22.6 us
    select_n x8, other arithmetic, turn(): return jax.tree.map(lambda a, b: jnp.where(reached, a, b), new, before)  18.5 us
  transfers between devices with their start and end apart: 7, of which 7 were waited for; matrix products, arithmetic and copies ran while one was open for 16% of the time, Pallas kernels for 0%

commit v1 on v0

v1 whole, which is shorter than its diff:
```python
import functools

import jax
import jax.numpy as jnp
from jax import lax
from jax.experimental import pallas as pl
from jax.experimental.pallas import tpu as pltpu
from jax.sharding import PartitionSpec as P

F32 = jnp.float32
BF16 = jnp.bfloat16
LANES = 128
HALO = 16
LIMIT = 40 * 1024 * 1024


def dot(a, b, dims=((1,), (0,)), precision=None):
    return lax.dot_general(
        a, b, (dims, ((), ())), precision=precision, preferred_element_type=F32
    )


TN = ((0,), (0,))
NT = ((1,), (1,))


def params():
    return pltpu.CompilerParams(vmem_limit_bytes=LIMIT)


def vmem(count):
    return [pl.BlockSpec(memory_space=pltpu.VMEM)] * count


def smem(count):
    return [pl.BlockSpec(memory_space=pltpu.SMEM)] * count


def shape(dims, dtype):
    return jax.ShapeDtypeStruct(dims, dtype)


def triangle(n):
    rows = lax.broadcasted_iota(jnp.int32, (n, n), 0)
    cols = lax.broadcasted_iota(jnp.int32, (n, n), 1)
    return rows >= cols


def vectors_kernel(dt_ref, bias_ref, alog_ref, step_ref, cum_ref, cumt_ref, grow_ref, endw_ref):
    raw = dt_ref[...] + bias_ref[...]
    step = jnp.maximum(raw, 0.0) + jnp.log1p(jnp.exp(-jnp.abs(raw)))
    log_decay = -step * jnp.exp(alog_ref[...])
    n = raw.shape[0]
    lower = jnp.where(triangle(n), 1.0, 0.0).astype(F32)
    cum = dot(lower, log_decay, precision=lax.Precision.HIGHEST)
    step_ref[...] = step
    cum_ref[...] = cum
    cumt_ref[...] = cum.T
    grow_ref[...] = jnp.exp(cum)
    endw_ref[...] = jnp.exp(cum[n - 1 : n, :] - cum)


def project_kernel(count, offs_ref, layer_ref, halo_ref, *refs):
    pieces = refs[:count]
    cw_ref, cb_ref, ext_ref, pre_ref, bc_ref = refs[count:]
    rows = pieces[0].shape[0]
    taps = cw_ref.shape[0]
    tokens = layer_ref.shape[0]
    total = jnp.zeros((tokens, pieces[0].shape[1]), F32)
    rim = jnp.zeros((HALO, pieces[0].shape[1]), F32)
    for k in range(count):
        at = pl.ds(pl.multiple_of(offs_ref[k], LANES), rows)
        w = pieces[k][...]
        total += dot(layer_ref[:, at], w)
        rim += dot(halo_ref[:, at], w)
    ext_ref[0:HALO, :] = rim
    ext_ref[HALO:, :] = total
    first = HALO - taps + 1
    pre = cb_ref[...] + cw_ref[0:1, :] * ext_ref[first : first + tokens, :]
    for k in range(1, taps):
        pre = pre + cw_ref[k : k + 1, :] * ext_ref[first + k : first + k + tokens, :]
    pre_ref[...] = pre
    bc_ref[...] = (pre * jax.nn.sigmoid(pre)).astype(BF16)


def widen(row, lane, heads):
    return jnp.concatenate(
        [jnp.broadcast_to(row[:, lane + h : lane + h + 1], (1, LANES)) for h in range(heads)], 1
    )


def states_kernel(
    heads, chunks, idx_ref, x0_ref, x1_ref, g0_ref, g1_ref, bc0_ref, bc1_ref, step_ref, grow_ref,
    endw_ref, *refs
):
    p_refs, q_refs = refs[:chunks], refs[chunks : 2 * chunks]
    sf_ref, ds_ref, dec_ref, s_scr, d_scr, dec_scr, xe_scr, ge_scr = refs[2 * chunks :]
    n = step_ref.shape[0]
    r = idx_ref[0]
    for slot, (x_ref, g_ref, bc_ref) in enumerate(
        ((x0_ref, g0_ref, bc0_ref), (x1_ref, g1_ref, bc1_ref))
    ):
        for h in range(heads):
            lane = slot * heads + h
            at = slice(h * LANES, (h + 1) * LANES)
            weight = step_ref[:, lane : lane + 1] * endw_ref[:, lane : lane + 1]
            xe_scr[:, at] = (x_ref[:, at].astype(F32) * weight).astype(BF16)
            ge_scr[:, at] = (g_ref[:, at].astype(F32) * grow_ref[:, lane : lane + 1]).astype(BF16)
        b = bc_ref[:, :LANES]
        c = bc_ref[:, LANES:]
        s_scr[slot] = dot(b, xe_scr[...], TN)
        d_scr[slot] = dot(c, ge_scr[...], TN)
        dec_scr[slot] = widen(grow_ref[n - 1 : n, :], slot * heads, heads)
    dec_first, dec_second = dec_scr[r], dec_scr[1 - r]
    s_first, d_second = s_scr[r], d_scr[1 - r]
    sf_ref[...] = s_first.astype(BF16)
    ds_ref[...] = d_second.astype(BF16)
    p = (dec_second * s_first + s_scr[1 - r]).astype(BF16)
    q = (dec_first * d_second + d_scr[r]).astype(BF16)
    width = p_refs[0].shape[1]
    for i in range(chunks):
        p_refs[i][...] = p[:, i * width : (i + 1) * width]
        q_refs[i][...] = q[:, i * width : (i + 1) * width]
    dec_ref[0:1, :] = dec_first * dec_second
    dec_ref[1:2, :] = dec_first
    dec_ref[2:3, :] = dec_second
    dec_ref[3:8, :] = jnp.zeros((5, dec_first.shape[1]), F32)


def final_kernel(
    heads, chunks, hops, idx_ref, x0_ref, x1_ref, g0_ref, g1_ref, bc0_ref, bc1_ref, step_ref,
    cum_ref, cumt_ref, grow_ref, endw_ref, dt_ref, bias_ref, alog_ref, skip_ref, sf_ref, ds_ref,
    dec_ref, *refs
):
    p_refs = refs[:chunks]
    e_refs = refs[chunks : chunks + chunks * hops]
    r_refs = refs[chunks + chunks * hops : chunks + 2 * chunks * hops]
    (
        y0_ref, y1_ref, dx0_ref, dx1_ref, dbc0_ref, dbc1_ref, draw_ref, sums_ref,
        e_scr, r_scr, n_scr, ce_scr, br_scr, xe_scr, ge_scr, gy_scr, ds_scr, re_scr,
    ) = refs[chunks + 2 * chunks * hops :]
    n = step_ref.shape[0]
    r = idx_ref[0]

    def whole(parts):
        columns = []
        for i in range(chunks):
            total = parts[i * hops][...].astype(F32)
            for k in range(1, hops):
                total = total + parts[i * hops + k][...].astype(F32)
            columns.append(total)
        return jnp.concatenate(columns, 1)

    dec_pair, dec_first, dec_second = dec_ref[0:1, :], dec_ref[1:2, :], dec_ref[2:3, :]
    entering = whole(e_refs)
    e_scr[r] = entering.astype(BF16)
    middle = dec_first * entering + sf_ref[...].astype(F32)
    e_scr[1 - r] = middle.astype(BF16)
    leaving = dec_pair * entering + jnp.concatenate([p[...] for p in p_refs], 1).astype(F32)
    later = whole(r_refs)
    r_scr[1 - r] = later.astype(BF16)
    earlier = dec_second * later + ds_ref[...].astype(F32)
    r_scr[r] = earlier.astype(BF16)
    n_scr[1 - r] = jnp.sum(later * leaving, axis=0, keepdims=True)
    n_scr[r] = jnp.sum(earlier * middle, axis=0, keepdims=True)

    mask = triangle(n)
    gy_scr[...] = jnp.zeros_like(gy_scr)
    ds_scr[...] = jnp.zeros_like(ds_scr)
    re_scr[...] = jnp.zeros_like(re_scr)
    for slot, (x_ref, g_ref, bc_ref, y_ref, dx_ref, dbc_ref) in enumerate(
        (
            (x0_ref, g0_ref, bc0_ref, y0_ref, dx0_ref, dbc0_ref),
            (x1_ref, g1_ref, bc1_ref, y1_ref, dx1_ref, dbc1_ref),
        )
    ):
        b = bc_ref[:, :LANES]
        c = bc_ref[:, LANES:]
        scores = dot(c, b, NT)
        e_all = e_scr[slot]
        r_all = r_scr[slot]
        ce_scr[...] = dot(c, e_all)
        br_scr[...] = dot(b, r_all)
        dscores = jnp.zeros((n, n), F32)
        for h in range(heads):
            lane = slot * heads + h
            at = slice(h * LANES, (h + 1) * LANES)
            step = step_ref[:, lane : lane + 1]
            grow = grow_ref[:, lane : lane + 1]
            endw = endw_ref[:, lane : lane + 1]
            gap = cum_ref[:, lane : lane + 1] - cumt_ref[lane : lane + 1, :]
            decay = jnp.exp(jnp.where(mask, gap, -jnp.inf))
            mixing = (scores * decay).astype(BF16)
            x = x_ref[:, at].astype(F32)
            g = g_ref[:, at]
            gf = g.astype(F32)
            xs = x * step
            xsb = xs.astype(BF16)
            xe_scr[:, at] = (xs * endw).astype(BF16)
            ge_scr[:, at] = (gf * grow).astype(BF16)
            skip = skip_ref[r * heads + h]
            y = dot(mixing, xsb) + grow * ce_scr[:, at]
            dxs = dot(mixing, g, TN) + endw * br_scr[:, at]
            dscores += dot(g, xsb, NT) * decay
            y_ref[:, at] = (y + skip * x).astype(BF16)
            dx_ref[:, at] = (dxs * step + skip * gf).astype(BF16)
            gy_scr[:, lane : lane + 1] = jnp.sum(gf * y, axis=1, keepdims=True)
            ds_scr[:, lane : lane + 1] = jnp.sum(x * dxs, axis=1, keepdims=True)
            re_scr[0:1, lane : lane + 1] = jnp.sum(n_scr[slot][:, at], axis=1, keepdims=True)
            re_scr[1:2, lane : lane + 1] = jnp.sum(
                jnp.sum(gf * x, axis=0, keepdims=True), axis=1, keepdims=True
            )
        dsb = dscores.astype(BF16)
        dbc_ref[:, :LANES] = dot(xe_scr[...], r_all, NT) + dot(dsb, c, TN)
        dbc_ref[:, LANES:] = dot(ge_scr[...], e_all, NT) + dot(dsb, b)

    step = step_ref[...]
    ds = ds_scr[...]
    rate = jnp.exp(alog_ref[...])
    last = lax.broadcasted_iota(jnp.int32, (n, LANES), 0) == n - 1
    dcum = gy_scr[...] - step * ds + jnp.where(last, re_scr[0:1, :], 0.0)
    lower = jnp.where(mask, 1.0, 0.0).astype(F32)
    dlog = dot(lower, dcum, TN, precision=lax.Precision.HIGHEST)
    draw = (ds - rate * dlog) * jax.nn.sigmoid(dt_ref[...] + bias_ref[...])
    draw_ref[...] = draw
    sums_ref[0:1, :] = jnp.sum(draw, axis=0, keepdims=True)
    sums_ref[1:2, :] = jnp.sum(dlog * (-step * rate), axis=0, keepdims=True)
    sums_ref[2:3, :] = re_scr[1:2, :]
    sums_ref[3:8, :] = jnp.zeros((5, LANES), F32)


def conv_back_kernel(own_ref, ret_ref, pre_ref, ext_ref, cw_ref, grad_ref, gradb_ref, sums_ref, z_scr):
    tokens = pre_ref.shape[0]
    taps = cw_ref.shape[0]
    pre = pre_ref[...]
    sig = jax.nn.sigmoid(pre)
    dconv = (own_ref[...] + ret_ref[...].astype(F32)) * sig * (1.0 + pre * (1.0 - sig))
    z_scr[...] = jnp.zeros_like(z_scr)
    z_scr[HALO : HALO + tokens, :] = dconv
    grad = cw_ref[0:1, :] * z_scr[taps - 1 : taps - 1 + tokens + HALO, :]
    for k in range(1, taps):
        grad = grad + cw_ref[k : k + 1, :] * z_scr[taps - 1 - k : taps - 1 - k + tokens + HALO, :]
    grad_ref[...] = grad
    gradb_ref[...] = grad.astype(BF16)
    sums_ref[...] = jnp.zeros_like(sums_ref)
    first = HALO - taps + 1
    for k in range(taps):
        sums_ref[k : k + 1, :] = jnp.sum(
            dconv * ext_ref[first + k : first + k + tokens, :], axis=0, keepdims=True
        )
    sums_ref[taps : taps + 1, :] = jnp.sum(dconv, axis=0, keepdims=True)


def pack_kernel(count, offs_ref, layer_ref, halo_ref, *outs):
    for k in range(count):
        rows = outs[k].shape[1]
        at = pl.ds(pl.multiple_of(offs_ref[k], LANES), rows)
        outs[k][0:HALO, :] = halo_ref[:, at]
        outs[k][HALO:, :] = layer_ref[:, at]


def weight_kernel(count, size, offs_ref, *refs):
    lefts, rights = refs[:count], refs[count : 2 * count]
    outs, total = refs[2 * count : 2 * count + size], refs[2 * count + size]
    acc = dot(lefts[0][...], rights[0][...], TN)
    for k in range(1, count):
        acc = acc + dot(lefts[k][...], rights[k][...], TN)
    total[...] = acc
    chunk = outs[0].shape[0]
    for k in range(size):
        at = pl.ds(pl.multiple_of(offs_ref[k], chunk), chunk)
        outs[k][...] = total[at, :].astype(BF16)


def place_rows_kernel(count, offs_ref, *refs):
    out = refs[count]
    chunk = refs[0].shape[0]
    for k in range(count):
        at = pl.ds(pl.multiple_of(offs_ref[k], chunk), chunk)
        out[at, :] = refs[k][...].astype(F32)


def tokens_kernel(count, offs_ref, grad_ref, rim_ref, *refs):
    pieces, out = refs[:count], refs[count]
    own = grad_ref[HALO:, :]
    tail = rim_ref.shape[0]
    g = jnp.concatenate([own[:-tail], own[-tail:] + rim_ref[...]], 0).astype(BF16)
    rows = pieces[0].shape[0]
    for k in range(count):
        at = pl.ds(pl.multiple_of(offs_ref[k], LANES), rows)
        out[:, at] = dot(g, pieces[k][...], NT).astype(BF16)


def toggled(x, axis, bits):
    size = lax.axis_size(axis)
    return lax.ppermute(x, axis, [(i, i ^ bits) for i in range(size)])


def everyone_sums(x, axis):
    bits = 1
    while bits < lax.axis_size(axis):
        x = x + toggled(x, axis, bits)
        bits *= 2
    return x


def chain(parts, decay, axis, forward):
    size = lax.axis_size(axis)
    pairs = size // 2
    received = [[] for _ in parts]
    width = parts[0].shape[1]
    for hop in range(pairs - 1):
        source = hop if forward else pairs - 1 - hop
        target = source + 1 if forward else source - 1
        lanes = [(2 * source + i, 2 * target + i) for i in range(2)]
        for i, part in enumerate(parts):
            value = part
            if hop:
                scale = decay[:, i * width : (i + 1) * width]
                value = (scale * received[i][-1].astype(F32) + part.astype(F32)).astype(BF16)
            received[i].append(lax.ppermute(value, axis, lanes))
    return received


def body(layer_in, w_bc, conv_w, conv_b, ssm_in, dt_raw, dt_bias, a_log, skip_scale, grad_out):
    ctx, fsdp = lax.axis_size("ctx"), lax.axis_size("fsdp")
    d, f = lax.axis_index("ctx"), lax.axis_index("fsdp")
    r = d % 2
    tokens_in, x, g, dt = layer_in[0], ssm_in[0], grad_out[0], dt_raw[0]
    tokens, width = x.shape
    total_heads = dt_bias.shape[0]
    heads = total_heads // 2
    half = width // 2
    state = w_bc.shape[1] // 2
    taps = conv_w.shape[0]
    rows = w_bc.shape[0]
    chunks = 2
    hops = ctx // 2 - 1
    idx = jnp.reshape(r, (1,)).astype(jnp.int32)
    column_offs = (jnp.arange(fsdp, dtype=jnp.int32) ^ f.astype(jnp.int32)) * rows
    chunk_rows = rows // ctx
    row_offs = (jnp.arange(ctx, dtype=jnp.int32) ^ d.astype(jnp.int32)) * chunk_rows

    def mine(a, axis=-1):
        n = a.shape[axis] // 2
        return jnp.where(
            r == 0, lax.slice_in_dim(a, 0, n, axis=axis), lax.slice_in_dim(a, n, 2 * n, axis=axis)
        )

    def other(a, axis=-1):
        n = a.shape[axis] // 2
        return jnp.where(
            r == 0, lax.slice_in_dim(a, n, 2 * n, axis=axis), lax.slice_in_dim(a, 0, n, axis=axis)
        )

    def joined(own, returned, axis=-1):
        return jnp.where(
            r == 0,
            jnp.concatenate([own, returned], axis),
            jnp.concatenate([returned, own], axis),
        )

    pieces = {0: w_bc}
    bit = fsdp // 2
    while bit:
        for k in list(pieces):
            pieces[k | bit] = toggled(pieces[k], "fsdp", bit)
        bit //= 2
    pieces = [pieces[k] for k in range(fsdp)]
    halo = lax.ppermute(tokens_in[tokens - HALO :], "ctx", [(i, i + 1) for i in range(ctx - 1)])
    x_recv = toggled(other(x), "ctx", 1)
    g_recv = toggled(other(g), "ctx", 1)
    dt_recv = toggled(other(dt), "ctx", 1)

    def lanes_of(a):
        return jnp.pad(a, ((0, 0), (0, LANES - a.shape[1])))

    def twice(a):
        m = mine(a)[None, :]
        return lanes_of(jnp.concatenate([m, m], 1))

    dt2 = lanes_of(jnp.concatenate([mine(dt), dt_recv], 1))
    bias2, alog2 = twice(dt_bias), twice(a_log)
    square = shape((tokens, LANES), F32)
    step, cum, cumt, grow, endw = pl.pallas_call(
        vectors_kernel,
        out_shape=[square] * 5,
        in_specs=vmem(3),
        out_specs=vmem(5),
        compiler_params=params(),
        name="vectors",
    )(dt2, bias2, alog2)

    ext, pre, bc = pl.pallas_call(
        functools.partial(project_kernel, fsdp),
        out_shape=[
            shape((tokens + HALO, 2 * state), F32),
            shape((tokens, 2 * state), F32),
            shape((tokens, 2 * state), BF16),
        ],
        in_specs=smem(1) + vmem(4 + fsdp),
        out_specs=vmem(3),
        compiler_params=params(),
        name="project",
    )(column_offs, tokens_in, halo, *pieces, conv_w, conv_b[None, :])
    bc_recv = toggled(bc, "ctx", 1)

    own_half = pl.BlockSpec((tokens, half), lambda i, at: (0, at[0]))

    def full(a):
        rank = len(a.shape)
        return pl.BlockSpec(a.shape, lambda i, at: (0,) * rank)

    part = shape((state, half // chunks), BF16)
    flat = shape((state, half), BF16)
    out_shape = [part] * (2 * chunks) + [flat, flat, shape((8, half), F32)]
    operands = (x, x_recv, g, g_recv, bc, bc_recv, step, grow, endw)
    in_specs = [own_half, full(x_recv), own_half, full(g_recv)] + [full(a) for a in operands[4:]]
    results = pl.pallas_call(
        functools.partial(states_kernel, heads, chunks),
        out_shape=out_shape,
        grid_spec=pltpu.PrefetchScalarGridSpec(
            num_scalar_prefetch=1,
            grid=(1,),
            in_specs=in_specs,
            out_specs=[full(a) for a in out_shape],
            scratch_shapes=[
                pltpu.VMEM((2, state, half), F32),
                pltpu.VMEM((2, state, half), F32),
                pltpu.VMEM((2, 1, half), F32),
                pltpu.VMEM((tokens, half), BF16),
                pltpu.VMEM((tokens, half), BF16),
            ],
        ),
        compiler_params=params(),
        name="states",
    )(idx, *operands)
    p_parts, q_parts = results[:chunks], results[chunks : 2 * chunks]
    s_first, d_second, decays = results[2 * chunks :]
    pair_decay = decays[0:1]
    received_e = chain(p_parts, pair_decay, "ctx", True)
    received_r = chain(q_parts, pair_decay, "ctx", False)

    late_tokens, late_halo, _ = lax.optimization_barrier((tokens_in, halo, bc))
    packs = pl.pallas_call(
        functools.partial(pack_kernel, fsdp),
        out_shape=[shape((tokens + HALO, rows), BF16)] * fsdp,
        in_specs=smem(1) + vmem(2),
        out_specs=vmem(fsdp),
        compiler_params=params(),
        name="pack",
    )(column_offs, late_tokens, late_halo)
    lefts = [packs[0]] + [toggled(packs[k], "fsdp", k) for k in range(1, fsdp)]

    out_shape = [shape((tokens, half), BF16)] * 4 + [shape((tokens, 2 * state), F32)] * 2
    out_shape += [square, shape((8, LANES), F32)]
    operands = (
        x, x_recv, g, g_recv, bc, bc_recv, step, cum, cumt, grow, endw, dt2, bias2, alog2,
        skip_scale, s_first, d_second, decays, *p_parts,
        *[a for group in received_e for a in group], *[a for group in received_r for a in group],
    )
    in_specs = [own_half, full(x_recv), own_half, full(g_recv)] + [full(a) for a in operands[4:]]
    in_specs[14] = pl.BlockSpec(memory_space=pltpu.SMEM)
    y_own, y_send, dx_own, dx_send, dbc_own, dbc_send, draw, head_sums = pl.pallas_call(
        functools.partial(final_kernel, heads, chunks, hops),
        out_shape=out_shape,
        grid_spec=pltpu.PrefetchScalarGridSpec(
            num_scalar_prefetch=1,
            grid=(1,),
            in_specs=in_specs,
            out_specs=[full(a) for a in out_shape],
            scratch_shapes=[
                pltpu.VMEM((2, state, half), BF16),
                pltpu.VMEM((2, state, half), BF16),
                pltpu.VMEM((2, 1, half), F32),
                pltpu.VMEM((tokens, half), F32),
                pltpu.VMEM((tokens, half), F32),
                pltpu.VMEM((tokens, half), BF16),
                pltpu.VMEM((tokens, half), BF16),
                pltpu.VMEM((tokens, LANES), F32),
                pltpu.VMEM((tokens, LANES), F32),
                pltpu.VMEM((8, LANES), F32),
            ],
        ),
        compiler_params=params(),
        name="final",
    )(idx, *operands)

    dbc_ret = toggled(dbc_send.astype(BF16), "ctx", 1)
    grad, grad_b, conv_sums = pl.pallas_call(
        conv_back_kernel,
        out_shape=[
            shape((tokens + HALO, 2 * state), F32),
            shape((tokens + HALO, 2 * state), BF16),
            shape((8, 2 * state), F32),
        ],
        in_specs=vmem(5),
        out_specs=vmem(3),
        scratch_shapes=[pltpu.VMEM((tokens + 2 * HALO, 2 * state), F32)],
        compiler_params=params(),
        name="conv_back",
    )(dbc_own, dbc_ret, pre, ext, conv_w)

    rights = [grad_b] + [toggled(grad_b, "fsdp", k) for k in range(1, fsdp)]
    terms = pl.pallas_call(
        functools.partial(weight_kernel, fsdp, ctx),
        out_shape=[shape((chunk_rows, 2 * state), BF16)] * ctx,
        in_specs=smem(1) + vmem(2 * fsdp),
        out_specs=vmem(ctx),
        scratch_shapes=[pltpu.VMEM((rows, 2 * state), F32)],
        compiler_params=params(),
        name="weight",
    )(row_offs, *lefts, *rights)
    total = terms[0].astype(F32)
    for k in range(1, ctx):
        total = total + toggled(terms[k], "ctx", k).astype(F32)
    total = total.astype(BF16)
    everyones = [total] + [toggled(total, "ctx", k) for k in range(1, ctx)]
    grad_weight = pl.pallas_call(
        functools.partial(place_rows_kernel, ctx),
        out_shape=shape((rows, 2 * state), F32),
        in_specs=smem(1) + vmem(ctx),
        out_specs=vmem(1)[0],
        compiler_params=params(),
        name="place_rows",
    )(row_offs, *everyones)

    both = head_sums[:3, :heads] + head_sums[:3, heads : 2 * heads]
    both = joined(both, jnp.zeros_like(both))
    both = jnp.pad(both.reshape(1, -1), ((0, 0), (0, 2 * state - 3 * total_heads)))
    small = jnp.concatenate([conv_sums[: taps + 1], both], 0)
    small = everyone_sums(everyone_sums(small, "fsdp"), "ctx")
    per_head = small[taps + 1, : 3 * total_heads].reshape(3, total_heads)

    rim = lax.ppermute(grad[HALO - 8 : HALO], "ctx", [(i + 1, i) for i in range(ctx - 1)])
    grad_tokens = pl.pallas_call(
        functools.partial(tokens_kernel, fsdp),
        out_shape=shape((tokens, fsdp * rows), BF16),
        in_specs=smem(1) + vmem(2 + fsdp),
        out_specs=vmem(1)[0],
        compiler_params=params(),
        name="grad_tokens",
    )(column_offs, grad, rim, *pieces)
    ssm_out = joined(y_own, toggled(y_send, "ctx", 1))
    grad_values = joined(dx_own, toggled(dx_send, "ctx", 1))
    grad_raw = joined(draw[:, :heads], toggled(draw[:, heads : 2 * heads], "ctx", 1))
    return (
        ssm_out[None],
        grad_values[None],
        grad_tokens[None],
        grad_raw[None],
        grad_weight,
        small[:taps],
        small[taps],
        per_head[0],
        per_head[1],
        per_head[2],
    )


def solution(mesh):
    tokens = P("fsdp", "ctx", None)
    in_specs = (tokens, P("fsdp", None), P(), P(), tokens, tokens, P(), P(), P(), tokens)
    out_specs = (tokens, tokens, tokens, tokens, P("fsdp", None), P(), P(), P(), P(), P())
    return jax.shard_map(body, mesh=mesh, in_specs=in_specs, out_specs=out_specs, check_vma=False)
```

time: 460 us -> 182 us (0.40)
  waiting for transfers between devices: 278 us -> 71.3 us
  blocking collectives: 62.4 us -> 0 us
  starting transfers between devices: 5.05 us -> 57.7 us
  other arithmetic: 42.4 us -> 8.16 us
  Pallas kernels: 0 us -> 28 us
  matrix products: 23.3 us -> 0 us
  local copies, waits for them, and re-layouts: 32.6 us -> 15.1 us
  between operations: 15.2 us -> 1.14 us
    all_gather x3 -> x0, waiting for transfers between devices: 199 us -> none  [the longest x1 97.2 us: carried_in(): lax.all_gather(a.astype(kind), axis)]
    ppermute x2 -> x50, waiting for transfers between devices: 6.98 us -> 71.3 us  [the longest x36 31.6 us: toggled(): return lax.ppermute(x, axis, [(i, i ^ bits) for i in range(size)])]
    ppermute x2 -> x50, starting transfers between devices: 4.66 us -> 57.7 us  [the longest x36 39.9 us: toggled(): return lax.ppermute(x, axis, [(i, i ^ bits) for i in range(size)])]
    psum x1 -> x0, blocking collectives: 39.8 us -> none  [body(): lax.psum((grad_cw, grad_cb, grad_bias, grad_log, grad_skip_local), ('ctx'...]
    reduce_scatter x1 -> x0, waiting for transfers between devices: 36.5 us -> none  [body(): lax.psum_scatter(lax.dot_general(columns, grad_rounded, (((0,), (0,)), ((...]
    psum x1 -> x0, waiting for transfers between devices: 34.5 us -> none  [body(): grad_weight = lax.psum(weight_part, 'ctx').astype(jnp.float32)]
    pallas_call x0 -> x9, Pallas kernels: none -> 28 us  [the longest x1 13.7 us: body(): pl.pallas_call(functools.partial(final_kernel, heads, chunks, hops), out_...]
    dot_general x14 -> x0, matrix products: 22.9 us -> none  [the longest x3 8.35 us: span_local(): jnp.einsum('hij,jhp->ihp', mixing, values, preferred_element_type=jnp.flo...]
  transfers between devices with their start and end apart: 7 -> 50, of which waited for: 7 -> 17; matrix products, arithmetic and copies ran while one was open for 16% -> 5% of each run, Pallas kernels for 0% -> 14%
where the time goes in v1:
time: 182 us; the launch traced here: 181 us
  waiting for transfers between devices  71.3 us (39%)
  starting transfers between devices  57.7 us (32%)
  Pallas kernels  28 us (15%)
  local copies, waits for them, and re-layouts  15.1 us (8%)
  other arithmetic  8.16 us (4%)
    ppermute x36, starting transfers between devices, toggled(): return lax.ppermute(x, axis, [(i, i ^ bits) for i in range(size)])  39.9 us
    ppermute x36, waiting for transfers between devices, toggled(): return lax.ppermute(x, axis, [(i, i ^ bits) for i in range(size)])  31.6 us
    ppermute x12, waiting for transfers between devices, chain(): received[i].append(lax.ppermute(value, axis, lanes))  19.2 us
    ppermute x1, waiting for transfers between devices, body(): lax.ppermute(tokens_in[tokens - HALO:], 'ctx', [(i, i + 1) for i in range...  16.6 us
    pallas_call x1, Pallas kernels, body(): pl.pallas_call(functools.partial(final_kernel, heads, chunks, hops), out_...  13.7 us
    ppermute x12, starting transfers between devices, chain(): received[i].append(lax.ppermute(value, axis, lanes))  13.1 us
    unnamed x72, local copies, waits for them, and re-layouts  12.1 us
    ppermute x1, waiting for transfers between devices, body(): lax.ppermute(grad[HALO - 8:HALO], 'ctx', [(i + 1, i) for i in range(ctx -...  3.99 us
  transfers between devices with their start and end apart: 50, of which 17 were waited for; matrix products, arithmetic and copies ran while one was open for 5% of the time, Pallas kernels for 14%

profile of v1, /device:TPU:0, one launch (start us, length us, event | category | flops | bytes accessed | tf_op | source)
XLA Modules:
  0.0 181.4 jit_solution(16811887401186474810)
XLA Ops:
  0.7 3.0 %collective-permute-start.4 = (bf16[1024,256]{1,0:T(8,128)(2,1)}, bf16[1024,256]{1,0:T(8,128)(2,1)S(1)}, u32[]{:S(2)}, u32[]{:S(2)}) collective-permute-start(bf16[1024,256]{1,0:T(8,128)(2,1)} %refs_0_.3), channel_id=1, source_target_pairs={{0,2},{1,3},{2,0},{3,1},{4,6},{5,7},{6,4},{7,5},{8,10},{9,11},{10,... | collective-permute-start | bytes 1572872 | tf_op jit(solution)/shard_map/ppermute | solution.py:296
  8.7 3.4 %collective-permute-start.2 = (bf16[16,4096]{1,0:T(8,128)(2,1)S(1)}, bf16[16,4096]{1,0:T(8,128)(2,1)S(1)}, u32[]{:S(2)}, u32[]{:S(2)}) collective-permute-start(bf16[16,4096]{1,0:T(8,128)(2,1)S(1)} %slice_bitcast_fusion), channel_id=1, source_target_pairs={{0,4},{4,8},{8,12},{12,16},{16,20},{20,24},{24,28},{1,5},{5,9},{9,... | collective-permute-start | bytes 393224 | tf_op jit(solution)/shard_map/ppermute | solution.py:370
  12.2 3.7 %collective-permute-done.4.refs_2_ = bf16[1024,256]{1,0:T(8,128)(2,1)S(1)} collective-permute-done((bf16[1024,256]{1,0:T(8,128)(2,1)}, bf16[1024,256]{1,0:T(8,128)(2,1)S(1)}, u32[]{:S(2)}, u32[]{:S(2)}) %collective-permute-start.4) | collective-permute-done | bytes 524320 | tf_op jit(solution)/shard_map/ppermute | solution.py:296
  16.9 16.6 %collective-permute-done.2.halo_ref = bf16[16,4096]{1,0:T(8,128)(2,1)S(1)} collective-permute-done((bf16[16,4096]{1,0:T(8,128)(2,1)S(1)}, bf16[16,4096]{1,0:T(8,128)(2,1)S(1)}, u32[]{:S(2)}, u32[]{:S(2)}) %collective-permute-start.2) | collective-permute-done | bytes 131104 | tf_op jit(solution)/shard_map/ppermute | solution.py:370
  33.4 2.5 %collective-permute-start.7 = (f32[128,16]{0,1:T(8,128)S(1)}, f32[128,16]{0,1:T(8,128)S(1)}, u32[]{:S(2)}, u32[]{:S(2)}) collective-permute-start(f32[128,16]{0,1:T(8,128)S(1)} %get-tuple-element.105), channel_id=1, source_target_pairs={{0,4},{4,0},{8,12},{12,8},{16,20},{20,16},{24,28},{28,24},{1,5},{5... | collective-permute-start | bytes 24584 | tf_op jit(solution)/shard_map/ppermute | solution.py:296
  43.6 3.8 %collective-permute-done.6.bc1_ref = bf16[128,256]{1,0:T(8,128)(2,1)S(1)} collective-permute-done((bf16[128,256]{1,0:T(8,128)(2,1)S(1)}, bf16[128,256]{1,0:T(8,128)(2,1)S(1)}, u32[]{:S(2)}, u32[]{:S(2)}) %collective-permute-start.6) | collective-permute-done | bytes 65568 | tf_op jit(solution)/shard_map/ppermute | solution.py:296
  47.4 3.5 %states.1 = (bf16[128,1024]{1,0:T(8,128)(2,1)S(1)}, bf16[128,1024]{1,0:T(8,128)(2,1)S(1)}, bf16[128,1024]{1,0:T(8,128)(2,1)S(1)}, bf16[128,1024]{1,0:T(8,128)(2,...) custom-call(s32[1]{0:T(128)} %bitcast.idx_ref, ...), custom_call_target="tpu_custom_call" | custom-call | tf_op jit(solution)/shard_map/states/pallas_call | solution.py:419
  50.9 3.5 %collective-permute-start.11 = (bf16[128,1024]{1,0:T(8,128)(2,1)S(1)}, bf16[128,1024]{1,0:T(8,128)(2,1)S(1)}, u32[]{:S(2)}, u32[]{:S(2)}) collective-permute-start(bf16[128,1024]{1,0:T(8,128)(2,1)S(1)} %get-tuple-element.60.refs_1_), channel_id=1, source_target_pairs={{0,8},{4,12},{1,9},{5,13},{2,10},{6,14},{3,11},{7,15}} | collective-permute-start | bytes 786440 | tf_op jit(solution)/shard_map/ppermute | solution.py:321
  57.1 4.0 %collective-permute-done.11.refs_5_ = bf16[128,1024]{1,0:T(8,128)(2,1)S(1)} collective-permute-done((bf16[128,1024]{1,0:T(8,128)(2,1)S(1)}, bf16[128,1024]{1,0:T(8,128)(2,1)S(1)}, u32[]{:S(2)}, u32[]{:S(2)}) %collective-permute-start.11) | collective-permute-done | bytes 262176 | tf_op jit(solution)/shard_map/ppermute | solution.py:321
  72.4 11.0 %collective-permute-done.19.refs_13_ = bf16[128,1024]{1,0:T(8,128)(2,1)S(1)} collective-permute-done((bf16[128,1024]{1,0:T(8,128)(2,1)S(1)}, bf16[128,1024]{1,0:T(8,128)(2,1)S(1)}, u32[]{:S(2)}, u32[]{:S(2)}) %collective-permute-start.19) | collective-permute-done | bytes 262176 | tf_op jit(solution)/shard_map/ppermute | solution.py:321
  83.4 2.8 %collective-permute-done.16.refs_10_ = bf16[128,1024]{1,0:T(8,128)(2,1)S(1)} collective-permute-done((bf16[128,1024]{1,0:T(8,128)(2,1)S(1)}, bf16[128,1024]{1,0:T(8,128)(2,1)S(1)}, u32[]{:S(2)}, u32[]{:S(2)}) %collective-permute-start.16) | collective-permute-done | bytes 262176 | tf_op jit(solution)/shard_map/ppermute | solution.py:321
  86.2 13.7 %final.1 = (bf16[128,2048]{1,0:T(8,128)(2,1)S(1)}, bf16[128,2048]{1,0:T(8,128)(2,1)S(1)}, bf16[128,2048]{1,0:T(8,128)(2,1)S(1)}, bf16[128,2048]{1,0:T(8,128)(2,1...) custom-call(s32[1]{0:T(128)} %bitcast.idx_ref, ...), custom_call_target="tpu_custom_call" | custom-call | tf_op jit(solution)/shard_map/final/pallas_call | solution.py:464
  102.3 3.9 %collective-permute-done.22.ret_ref = bf16[128,256]{1,0:T(8,128)(2,1)S(1)} collective-permute-done((bf16[128,256]{1,0:T(8,128)(2,1)S(1)}, bf16[128,256]{1,0:T(8,128)(2,1)S(1)}, u32[]{:S(2)}, u32[]{:S(2)}) %collective-permute-start.22) | collective-permute-done | bytes 65568 | tf_op jit(solution)/shard_map/ppermute | solution.py:296
  113.3 12.5 %collective-permute-done.46 = f32[6,256]{1,0:T(8,128)S(1)} collective-permute-done((f32[6,256]{1,0:T(8,128)S(1)}, f32[6,256]{1,0:T(8,128)S(1)}, u32[]{:S(2)}, u32[]{:S(2)}) %collective-permute-start.46) | collective-permute-done | bytes 6176 | tf_op jit(solution)/shard_map/ppermute | solution.py:296
  127.0 2.7 %collective-permute-done.30.refs_7_ = bf16[144,256]{1,0:T(8,128)(2,1)S(1)} collective-permute-done((bf16[144,256]{1,0:T(8,128)(2,1)S(1)}, bf16[144,256]{1,0:T(8,128)(2,1)S(1)}, u32[]{:S(2)}, u32[]{:S(2)}) %collective-permute-start.30) | collective-permute-done | bytes 73760 | tf_op jit(solution)/shard_map/ppermute | solution.py:296
  129.7 2.6 %weight.1 = (bf16[128,256]{1,0:T(8,128)(2,1)S(1)}, bf16[128,256]{1,0:T(8,128)(2,1)S(1)}, bf16[128,256]{1,0:T(8,128)(2,1)S(1)}, bf16[128,256]{1,0:T(8,128)(2,1)},...) custom-call(s32[8]{0:T(128)S(1)} %xor_multiply_fusion.offs_ref, ...), custom_call_target="tpu_custom_call" | custom-call | tf_op jit(solution)/shard_map/weight/pallas_call | solution.py:505
  137.2 3.1 %collective-permute-start.34 = (bf16[128,256]{1,0:T(8,128)(2,1)S(1)}, bf16[128,256]{1,0:T(8,128)(2,1)}, u32[]{:S(2)}, u32[]{:S(2)}) collective-permute-start(bf16[128,256]{1,0:T(8,128)(2,1)S(1)} %get-tuple-element.84), channel_id=1, source_target_pairs={{0,16},{4,20},{8,24},{12,28},{16,0},{20,4},{24,8},{28,12},{1,17},{... | collective-permute-start | bytes 196616 | tf_op jit(solution)/shard_map/ppermute | solution.py:296
  141.7 2.4 %collective-permute-start.36 = (bf16[128,256]{1,0:T(8,128)(2,1)S(1)}, bf16[128,256]{1,0:T(8,128)(2,1)S(1)}, u32[]{:S(2)}, u32[]{:S(2)}) collective-permute-start(bf16[128,256]{1,0:T(8,128)(2,1)S(1)} %get-tuple-element.86), channel_id=1, source_target_pairs={{0,24},{4,28},{8,16},{12,20},{16,8},{20,12},{24,0},{28,4},{1,25},{... | collective-permute-start | bytes 196616 | tf_op jit(solution)/shard_map/ppermute | solution.py:296
  154.3 2.5 %collective-permute-start.39 = (bf16[128,256]{1,0:T(8,128)(2,1)S(1)}, bf16[128,256]{1,0:T(8,128)(2,1)S(1)}, u32[]{:S(2)}, u32[]{:S(2)}) collective-permute-start(bf16[128,256]{1,0:T(8,128)(2,1)S(1)} %add_convert_fusion.refs_0_), channel_id=1, source_target_pairs={{0,8},{4,12},{8,0},{12,4},{16,24},{20,28},{24,16},{28,20},{1,9},{5... | collective-permute-start | bytes 196616 | tf_op jit(solution)/shard_map/ppermute | solution.py:296
  156.8 4.0 %collective-permute-done.23.rim_ref = f32[8,256]{1,0:T(8,128)S(1)} collective-permute-done((f32[8,256]{1,0:T(8,128)S(1)}, f32[8,256]{1,0:T(8,128)S(1)}, u32[]{:S(2)}, u32[]{:S(2)}) %collective-permute-start.23) | collective-permute-done | bytes 8224 | tf_op jit(solution)/shard_map/ppermute | solution.py:535
  162.4 2.9 %grad_tokens.1 = bf16[128,4096]{1,0:T(8,128)(2,1)} custom-call(s32[4]{0:T(128)S(1)} %xor_multiply_fusion.1.offs_ref, f32[144,256]{1,0:T(8,128)S(1)} %get-tuple-element.71.grad_ref, f32[8,256]{1,0:T(8,128)S(1)} %collective-permute-done.23.rim_ref, bf16[1024,256]{1,0:T(8,128)(2,1)S(1)} %copy-done.4, bf16[1024,256]{1,0:T(8,128)(2,1)S(1)} %copy-done.10, ...), custom_call_target="tpu_custom_call" | custom-call | tf_op jit(solution)/shard_map/grad_tokens/pallas_call | solution.py:536
  165.3 2.5 %collective-permute-start.20 = (bf16[128,2048]{1,0:T(8,128)(2,1)S(1)}, bf16[128,2048]{1,0:T(8,128)(2,1)S(1)}, u32[]{:S(2)}, u32[]{:S(2)}) collective-permute-start(bf16[128,2048]{1,0:T(8,128)(2,1)S(1)} %copy-done.27), channel_id=1, source_target_pairs={{0,4},{4,0},{8,12},{12,8},{16,20},{20,16},{24,28},{28,24},{1,5},{5... | collective-permute-start | bytes 1572872 | tf_op jit(solution)/shard_map/ppermute | solution.py:296
  170.3 2.6 %collective-permute-start.44 = (bf16[128,256]{1,0:T(8,128)(2,1)S(1)}, bf16[128,256]{1,0:T(8,128)(2,1)S(1)}, u32[]{:S(2)}, u32[]{:S(2)}) collective-permute-start(bf16[128,256]{1,0:T(8,128)(2,1)S(1)} %add_convert_fusion.refs_0_), channel_id=1, source_target_pairs={{0,28},{4,24},{8,20},{12,16},{16,12},{20,8},{24,4},{28,0},{1,29},{... | collective-permute-start | bytes 196616 | tf_op jit(solution)/shard_map/ppermute | solution.py:296
  174.8 2.5 %collective-permute-done.44.refs_7_ = bf16[128,256]{1,0:T(8,128)(2,1)S(1)} collective-permute-done((bf16[128,256]{1,0:T(8,128)(2,1)S(1)}, bf16[128,256]{1,0:T(8,128)(2,1)S(1)}, u32[]{:S(2)}, u32[]{:S(2)}) %collective-permute-start.44) | collective-permute-done | bytes 65568 | tf_op jit(solution)/shard_map/ppermute | solution.py:296
  (195 shorter events, 64.6 us)
Async XLA Ops:
  0.7 15.2 %collective-permute-start.4 = (bf16[1024,256]{1,0:T(8,128)(2,1)}, bf16[1024,256]{1,0:T(8,128)(2,1)S(1)}, u32[]{:S(2)}, u32[]{:S(2)}) collective-permute-start(bf16[1024,256]{1,0:T(8,128)(2,1)} %refs_0_.3), channel_id=1, source_target_pairs={{0,2},{1,3},{2,0},{3,1},{4,6},{5,7},{6,4},{7,5},{8,10},{9,11},{10,... | collective-permute-start | bytes 1572872 | tf_op jit(solution)/shard_map/ppermute | solution.py:296
  3.7 32.2 %collective-permute-start.3 = (bf16[1024,256]{1,0:T(8,128)(2,1)}, bf16[1024,256]{1,0:T(8,128)(2,1)S(1)}, u32[]{:S(2)}, u32[]{:S(2)}) collective-permute-start(bf16[1024,256]{1,0:T(8,128)(2,1)} %refs_0_.3), channel_id=1, source_target_pairs={{0,1},{1,0},{2,3},{3,2},{4,5},{5,4},{6,7},{7,6},{8,9},{9,8},{10,11... | collective-permute-start | bytes 1572872 | tf_op jit(solution)/shard_map/ppermute | solution.py:296
  5.8 37.8 %collective-permute-start = (bf16[128,2048]{1,0:T(8,128)(2,1)}, bf16[128,2048]{1,0:T(8,128)(2,1)}, u32[]{:S(2)}, u32[]{:S(2)}) collective-permute-start(bf16[128,2048]{1,0:T(8,128)(2,1)} %slice_select_fusion.1), channel_id=1, source_target_pairs={{0,4},{4,0},{8,12},{12,8},{16,20},{20,16},{24,28},{28,24},{1,5},{5... | collective-permute-start | bytes 1572872 | tf_op jit(solution)/shard_map/ppermute | solution.py:296
  8.2 35.4 %collective-permute-start.1 = (bf16[128,2048]{1,0:T(8,128)(2,1)}, bf16[128,2048]{1,0:T(8,128)(2,1)}, u32[]{:S(2)}, u32[]{:S(2)}) collective-permute-start(bf16[128,2048]{1,0:T(8,128)(2,1)} %slice_select_fusion), channel_id=1, source_target_pairs={{0,4},{4,0},{8,12},{12,8},{16,20},{20,16},{24,28},{28,24},{1,5},{5... | collective-permute-start | bytes 1572872 | tf_op jit(solution)/shard_map/ppermute | solution.py:296
  8.7 24.7 %collective-permute-start.2 = (bf16[16,4096]{1,0:T(8,128)(2,1)S(1)}, bf16[16,4096]{1,0:T(8,128)(2,1)S(1)}, u32[]{:S(2)}, u32[]{:S(2)}) collective-permute-start(bf16[16,4096]{1,0:T(8,128)(2,1)S(1)} %slice_bitcast_fusion), channel_id=1, source_target_pairs={{0,4},{4,8},{8,12},{12,16},{16,20},{20,24},{24,28},{1,5},{5,9},{9,... | collective-permute-start | bytes 393224 | tf_op jit(solution)/shard_map/ppermute | solution.py:370
  15.8 20.9 %collective-permute-start.5 = (bf16[1024,256]{1,0:T(8,128)(2,1)S(1)}, bf16[1024,256]{1,0:T(8,128)(2,1)}, u32[]{:S(2)}, u32[]{:S(2)}) collective-permute-start(bf16[1024,256]{1,0:T(8,128)(2,1)S(1)} %collective-permute-done.4.refs_2_), channel_id=1, source_target_pairs={{0,1},{1,0},{2,3},{3,2},{4,5},{5,4},{6,7},{7,6},{8,9},{9,8},{10,11... | collective-permute-start | bytes 1572872 | tf_op jit(solution)/shard_map/ppermute | solution.py:296
  66.5 16.9 %collective-permute-start.19 = (bf16[128,1024]{1,0:T(8,128)(2,1)S(1)}, bf16[128,1024]{1,0:T(8,128)(2,1)S(1)}, u32[]{:S(2)}, u32[]{:S(2)}) collective-permute-start(bf16[128,1024]{1,0:T(8,128)(2,1)S(1)} %get-tuple-element.109), channel_id=1, source_target_pairs={{8,0},{12,4},{9,1},{13,5},{10,2},{14,6},{11,3},{15,7}} | collective-permute-start | bytes 786440 | tf_op jit(solution)/shard_map/ppermute | solution.py:321
  68.1 15.3 %collective-permute-start.10 = (bf16[128,1024]{1,0:T(8,128)(2,1)S(1)}, bf16[128,1024]{1,0:T(8,128)(2,1)S(1)}, u32[]{:S(2)}, u32[]{:S(2)}) collective-permute-start(bf16[128,1024]{1,0:T(8,128)(2,1)S(1)} %get-tuple-element.114), channel_id=1, source_target_pairs={{16,24},{20,28},{17,25},{21,29},{18,26},{22,30},{19,27},{23,31}} | collective-permute-start | bytes 786440 | tf_op jit(solution)/shard_map/ppermute | solution.py:321
  68.8 17.4 %collective-permute-start.16 = (bf16[128,1024]{1,0:T(8,128)(2,1)S(1)}, bf16[128,1024]{1,0:T(8,128)(2,1)S(1)}, u32[]{:S(2)}, u32[]{:S(2)}) collective-permute-start(bf16[128,1024]{1,0:T(8,128)(2,1)S(1)} %get-tuple-element.113), channel_id=1, source_target_pairs={{8,0},{12,4},{9,1},{13,5},{10,2},{14,6},{11,3},{15,7}} | collective-permute-start | bytes 786440 | tf_op jit(solution)/shard_map/ppermute | solution.py:321
  72.3 39.5 %collective-permute-start.25 = (bf16[144,1024]{1,0:T(8,128)(2,1)}, bf16[144,1024]{1,0:T(8,128)(2,1)}, u32[]{:S(2)}, u32[]{:S(2)}) collective-permute-start(bf16[144,1024]{1,0:T(8,128)(2,1)} %get-tuple-element.76), channel_id=1, source_target_pairs={{0,1},{1,0},{2,3},{3,2},{4,5},{5,4},{6,7},{7,6},{8,9},{9,8},{10,11... | collective-permute-start | bytes 884744 | tf_op jit(solution)/shard_map/ppermute | solution.py:296
  109.3 16.6 %collective-permute-start.26 = (bf16[144,1024]{1,0:T(8,128)(2,1)}, bf16[144,1024]{1,0:T(8,128)(2,1)S(1)}, u32[]{:S(2)}, u32[]{:S(2)}) collective-permute-start(bf16[144,1024]{1,0:T(8,128)(2,1)} %copy-done.30), channel_id=1, source_target_pairs={{0,2},{1,3},{2,0},{3,1},{4,6},{5,7},{6,4},{7,5},{8,10},{9,11},{10,... | collective-permute-start | bytes 884744 | tf_op jit(solution)/shard_map/ppermute | solution.py:296
  109.9 16.1 %collective-permute-start.27 = (bf16[144,1024]{1,0:T(8,128)(2,1)}, bf16[144,1024]{1,0:T(8,128)(2,1)S(1)}, u32[]{:S(2)}, u32[]{:S(2)}) collective-permute-start(bf16[144,1024]{1,0:T(8,128)(2,1)} %copy-done.29), channel_id=1, source_target_pairs={{0,3},{1,2},{2,1},{3,0},{4,7},{5,6},{6,5},{7,4},{8,11},{9,10},{10,... | collective-permute-start | bytes 884744 | tf_op jit(solution)/shard_map/ppermute | solution.py:296
  111.2 14.7 %collective-permute-start.46 = (f32[6,256]{1,0:T(8,128)S(1)}, f32[6,256]{1,0:T(8,128)S(1)}, u32[]{:S(2)}, u32[]{:S(2)}) collective-permute-start(f32[6,256]{1,0:T(8,128)S(1)} %fusion.11), channel_id=1, source_target_pairs={{0,2},{1,3},{2,0},{3,1},{4,6},{5,7},{6,4},{7,5},{8,10},{9,11},{10,... | collective-permute-start | bytes 18440 | tf_op jit(solution)/shard_map/ppermute | solution.py:296
  111.8 14.3 %collective-permute-start.28 = (bf16[144,256]{1,0:T(8,128)(2,1)S(1)}, bf16[144,256]{1,0:T(8,128)(2,1)S(1)}, u32[]{:S(2)}, u32[]{:S(2)}) collective-permute-start(bf16[144,256]{1,0:T(8,128)(2,1)S(1)} %get-tuple-element.79.refs_4_), channel_id=1, source_target_pairs={{0,1},{1,0},{2,3},{3,2},{4,5},{5,4},{6,7},{7,6},{8,9},{9,8},{10,11... | collective-permute-start | bytes 221192 | tf_op jit(solution)/shard_map/ppermute | solution.py:296
  111.8 15.2 %collective-permute-start.29 = (bf16[144,256]{1,0:T(8,128)(2,1)S(1)}, bf16[144,256]{1,0:T(8,128)(2,1)S(1)}, u32[]{:S(2)}, u32[]{:S(2)}) collective-permute-start(bf16[144,256]{1,0:T(8,128)(2,1)S(1)} %get-tuple-element.79.refs_4_), channel_id=1, source_target_pairs={{0,2},{1,3},{2,0},{3,1},{4,6},{5,7},{6,4},{7,5},{8,10},{9,11},{10,... | collective-permute-start | bytes 221192 | tf_op jit(solution)/shard_map/ppermute | solution.py:296
  132.3 11.9 %collective-permute-start.32 = (bf16[128,256]{1,0:T(8,128)(2,1)S(1)}, bf16[128,256]{1,0:T(8,128)(2,1)S(1)}, u32[]{:S(2)}, u32[]{:S(2)}) collective-permute-start(bf16[128,256]{1,0:T(8,128)(2,1)S(1)} %get-tuple-element.82), channel_id=1, source_target_pairs={{0,8},{4,12},{8,0},{12,4},{16,24},{20,28},{24,16},{28,20},{1,9},{5... | collective-permute-start | bytes 196616 | tf_op jit(solution)/shard_map/ppermute | solution.py:296
  136.4 10.3 %collective-permute-start.33 = (bf16[128,256]{1,0:T(8,128)(2,1)}, bf16[128,256]{1,0:T(8,128)(2,1)S(1)}, u32[]{:S(2)}, u32[]{:S(2)}) collective-permute-start(bf16[128,256]{1,0:T(8,128)(2,1)} %get-tuple-element.83), channel_id=1, source_target_pairs={{0,12},{4,8},{8,4},{12,0},{16,28},{20,24},{24,20},{28,16},{1,13},{... | collective-permute-start | bytes 196616 | tf_op jit(solution)/shard_map/ppermute | solution.py:296
  137.2 10.9 %collective-permute-start.34 = (bf16[128,256]{1,0:T(8,128)(2,1)S(1)}, bf16[128,256]{1,0:T(8,128)(2,1)}, u32[]{:S(2)}, u32[]{:S(2)}) collective-permute-start(bf16[128,256]{1,0:T(8,128)(2,1)S(1)} %get-tuple-element.84), channel_id=1, source_target_pairs={{0,16},{4,20},{8,24},{12,28},{16,0},{20,4},{24,8},{28,12},{1,17},{... | collective-permute-start | bytes 196616 | tf_op jit(solution)/shard_map/ppermute | solution.py:296
  146.7 32.2 %collective-permute-start.21 = (bf16[128,2048]{1,0:T(8,128)(2,1)}, bf16[128,2048]{1,0:T(8,128)(2,1)S(1)}, u32[]{:S(2)}, u32[]{:S(2)}) collective-permute-start(bf16[128,2048]{1,0:T(8,128)(2,1)} %copy-done.28), channel_id=1, source_target_pairs={{0,4},{4,0},{8,12},{12,8},{16,20},{20,16},{24,28},{28,24},{1,5},{5... | collective-permute-start | bytes 1572872 | tf_op jit(solution)/shard_map/ppermute | solution.py:296
  148.1 12.7 %collective-permute-start.23 = (f32[8,256]{1,0:T(8,128)S(1)}, f32[8,256]{1,0:T(8,128)S(1)}, u32[]{:S(2)}, u32[]{:S(2)}) collective-permute-start(f32[8,256]{1,0:T(8,128)S(1)} %slice.107), channel_id=1, source_target_pairs={{4,0},{8,4},{12,8},{16,12},{20,16},{24,20},{28,24},{5,1},{9,5},{13... | collective-permute-start | bytes 24584 | tf_op jit(solution)/shard_map/ppermute | solution.py:535
  149.6 11.2 %collective-permute-start.49 = (f32[6,256]{1,0:T(8,128)S(1)}, f32[6,256]{1,0:T(8,128)S(1)}, u32[]{:S(2)}, u32[]{:S(2)}) collective-permute-start(f32[6,256]{1,0:T(8,128)S(1)} %add.99), channel_id=1, source_target_pairs={{0,16},{4,20},{8,24},{12,28},{16,0},{20,4},{24,8},{28,12},{1,17},{... | collective-permute-start | bytes 18440 | tf_op jit(solution)/shard_map/ppermute | solution.py:296
  152.8 12.4 %collective-permute-start.38 = (bf16[128,256]{1,0:T(8,128)(2,1)S(1)}, bf16[128,256]{1,0:T(8,128)(2,1)S(1)}, u32[]{:S(2)}, u32[]{:S(2)}) collective-permute-start(bf16[128,256]{1,0:T(8,128)(2,1)S(1)} %add_convert_fusion.refs_0_), channel_id=1, source_target_pairs={{0,4},{4,0},{8,12},{12,8},{16,20},{20,16},{24,28},{28,24},{1,5},{5... | collective-permute-start | bytes 196616 | tf_op jit(solution)/shard_map/ppermute | solution.py:296
  154.3 13.6 %collective-permute-start.39 = (bf16[128,256]{1,0:T(8,128)(2,1)S(1)}, bf16[128,256]{1,0:T(8,128)(2,1)S(1)}, u32[]{:S(2)}, u32[]{:S(2)}) collective-permute-start(bf16[128,256]{1,0:T(8,128)(2,1)S(1)} %add_convert_fusion.refs_0_), channel_id=1, source_target_pairs={{0,8},{4,12},{8,0},{12,4},{16,24},{20,28},{24,16},{28,20},{1,9},{5... | collective-permute-start | bytes 196616 | tf_op jit(solution)/shard_map/ppermute | solution.py:296
  165.3 14.9 %collective-permute-start.20 = (bf16[128,2048]{1,0:T(8,128)(2,1)S(1)}, bf16[128,2048]{1,0:T(8,128)(2,1)S(1)}, u32[]{:S(2)}, u32[]{:S(2)}) collective-permute-start(bf16[128,2048]{1,0:T(8,128)(2,1)S(1)} %copy-done.27), channel_id=1, source_target_pairs={{0,4},{4,0},{8,12},{12,8},{16,20},{20,16},{24,28},{28,24},{1,5},{5... | collective-permute-start | bytes 1572872 | tf_op jit(solution)/shard_map/ppermute | solution.py:296
  (62 other events, 554.2 us)

commit v2 on v1

v2 whole, which is shorter than its diff:
```python
import functools

import jax
import jax.numpy as jnp
from jax import lax
from jax.experimental import pallas as pl
from jax.experimental.pallas import tpu as pltpu
from jax.sharding import PartitionSpec as P

F32 = jnp.float32
BF16 = jnp.bfloat16
LANES = 128
HALO = 16
GROUPS = 2
CHUNKS = 1
LIMIT = 16 * 1024 * 1024
HIGHEST = lax.Precision.HIGHEST
TN = ((0,), (0,))
NT = ((1,), (1,))


def dot(a, b, dims=((1,), (0,)), precision=None):
    return lax.dot_general(
        a, b, (dims, ((), ())), precision=precision, preferred_element_type=F32
    )


def shape(dims, dtype):
    return jax.ShapeDtypeStruct(dims, dtype)


def call(kernel, name, out_shape, smem, *operands, scratch=(), flops=0):
    single = not isinstance(out_shape, list)
    outs = [out_shape] if single else out_shape
    moved = sum(a.size * a.dtype.itemsize for a in [*operands, *outs])
    result = pl.pallas_call(
        kernel,
        out_shape=outs,
        in_specs=[pl.BlockSpec(memory_space=pltpu.SMEM)] * len(smem)
        + [pl.BlockSpec(memory_space=pltpu.VMEM)] * len(operands),
        out_specs=[pl.BlockSpec(memory_space=pltpu.VMEM)] * len(outs),
        scratch_shapes=list(scratch),
        compiler_params=pltpu.CompilerParams(vmem_limit_bytes=LIMIT),
        cost_estimate=pl.CostEstimate(flops=flops, bytes_accessed=moved, transcendentals=0),
        name=name,
    )(*smem, *operands)
    return result[0] if single else result


def aligned(at, size):
    return pl.ds(pl.multiple_of(at, LANES), size)


def triangle(n):
    rows = lax.broadcasted_iota(jnp.int32, (n, n), 0)
    cols = lax.broadcasted_iota(jnp.int32, (n, n), 1)
    return rows >= cols


def split(value):
    high = value.astype(BF16)
    return high, (value - high.astype(F32)).astype(BF16)


def swap_kernel(offs_ref, x_ref, g_ref, *refs):
    outs, sems = refs[:GROUPS], refs[GROUPS]
    width = outs[0].shape[1] // 2
    copies = []
    for i in range(GROUPS):
        for j, source in enumerate((x_ref, g_ref)):
            copies.append(
                pltpu.make_async_copy(
                    source.at[:, aligned(offs_ref[0] + i * width, width)],
                    outs[i].at[:, j * width : (j + 1) * width],
                    sems.at[2 * i + j],
                )
            )
    for copy in copies:
        copy.start()
    for copy in copies:
        copy.wait()


def vectors_kernel(dt_ref, bias_ref, alog_ref, step_ref, cum_ref, cumt_ref, grow_ref, endw_ref):
    raw = dt_ref[...] + bias_ref[...]
    step = jnp.maximum(raw, 0.0) + jnp.log1p(jnp.exp(-jnp.abs(raw)))
    log_decay = -step * jnp.exp(alog_ref[...])
    n = raw.shape[0]
    lower = jnp.where(triangle(n), 1.0, 0.0).astype(F32)
    cum = dot(lower, log_decay, precision=HIGHEST)
    step_ref[...] = step
    cum_ref[...] = cum
    cumt_ref[...] = cum.T
    grow_ref[...] = jnp.exp(cum)
    endw_ref[...] = jnp.exp(cum[n - 1 : n, :] - cum)


def project_kernel(count, offs_ref, layer_ref, halo_ref, *refs):
    pieces = refs[:count]
    cw_ref, cb_ref, ext_ref, pre_ref, bc_ref = refs[count:]
    rows = pieces[0].shape[0]
    taps = cw_ref.shape[0]
    tokens = layer_ref.shape[0]
    total = jnp.zeros((tokens, pieces[0].shape[1]), F32)
    rim = jnp.zeros((HALO, pieces[0].shape[1]), F32)
    for k in range(count):
        at = aligned(offs_ref[k], rows)
        w = pieces[k][...]
        total += dot(layer_ref[:, at], w)
        rim += dot(halo_ref[:, at], w)
    ext_ref[0:HALO, :] = rim
    ext_ref[HALO:, :] = total
    first = HALO - taps + 1
    pre = cb_ref[...] + cw_ref[0:1, :] * ext_ref[first : first + tokens, :]
    for k in range(1, taps):
        pre = pre + cw_ref[k : k + 1, :] * ext_ref[first + k : first + k + tokens, :]
    pre_ref[...] = pre
    bc_ref[...] = (pre * jax.nn.sigmoid(pre)).astype(BF16)


def scale_kernel(heads, lane, offs_ref, x_ref, g_ref, step_ref, grow_ref, endw_ref, xe_ref, ge_ref):
    for h in range(heads):
        at = slice(h * LANES, (h + 1) * LANES)
        one = slice(lane + h, lane + h + 1)
        x = x_ref[:, aligned(offs_ref[0] + h * LANES, LANES)].astype(F32)
        g = g_ref[:, aligned(offs_ref[1] + h * LANES, LANES)].astype(F32)
        xe_ref[:, at] = (x * (step_ref[:, one] * endw_ref[:, one])).astype(BF16)
        ge_ref[:, at] = (g * grow_ref[:, one]).astype(BF16)


def widen(row, lane, heads):
    return jnp.concatenate(
        [jnp.broadcast_to(row[:, lane + h : lane + h + 1], (1, LANES)) for h in range(heads)], 1
    )


def states_kernel(
    heads, lanes, idx_ref, bc0_ref, bc1_ref, xe0_ref, ge0_ref, xe1_ref, ge1_ref, grow_ref,
    p_ref, q_ref, sf_ref, ds_ref, dec_ref, s_scr, d_scr, dec_scr,
):
    n = grow_ref.shape[0]
    r = idx_ref[0]
    for slot, (bc_ref, xe_ref, ge_ref) in enumerate(
        ((bc0_ref, xe0_ref, ge0_ref), (bc1_ref, xe1_ref, ge1_ref))
    ):
        s_scr[slot] = dot(bc_ref[:, :LANES], xe_ref[...], TN)
        d_scr[slot] = dot(bc_ref[:, LANES:], ge_ref[...], TN)
        dec_scr[slot] = widen(grow_ref[n - 1 : n, :], lanes[slot], heads)
    dec_first, dec_second = dec_scr[r], dec_scr[1 - r]
    s_first, d_second = s_scr[r], d_scr[1 - r]
    sf_ref[...] = s_first.astype(BF16)
    ds_ref[...] = d_second.astype(BF16)
    p_ref[...] = (dec_second * s_first + s_scr[1 - r]).astype(BF16)
    q_ref[...] = (dec_first * d_second + d_scr[r]).astype(BF16)
    dec_ref[0:1, :] = dec_first * dec_second
    dec_ref[1:2, :] = dec_first
    dec_ref[2:3, :] = dec_second
    dec_ref[3:8, :] = jnp.zeros((5, dec_first.shape[1]), F32)


def inside_kernel(
    heads, lane, skip_at, idx_ref, offs_ref, skip_ref, x_ref, g_ref, bc_ref, step_ref, cum_ref,
    cumt_ref, y_ref, dx_ref, dscores_ref, gy_ref, ds_ref, gx_ref,
):
    n = step_ref.shape[0]
    mask = triangle(n)
    scores = jnp.where(mask, dot(bc_ref[:, LANES:], bc_ref[:, :LANES], NT), 0.0)
    gy_ref[...] = jnp.zeros_like(gy_ref)
    ds_ref[...] = jnp.zeros_like(ds_ref)
    gx_ref[...] = jnp.zeros_like(gx_ref)
    dscores = jnp.zeros((n, n), F32)
    for h in range(heads):
        at = slice(h * LANES, (h + 1) * LANES)
        one = slice(lane + h, lane + h + 1)
        step = step_ref[:, one]
        gap = cum_ref[:, one] - cumt_ref[one, :]
        decay = jnp.exp(jnp.where(mask, gap, 0.0))
        mixing = (scores * decay).astype(BF16)
        x = x_ref[:, aligned(offs_ref[0] + h * LANES, LANES)].astype(F32)
        g = g_ref[:, aligned(offs_ref[1] + h * LANES, LANES)]
        gf = g.astype(F32)
        xs = (x * step).astype(BF16)
        skip = skip_ref[idx_ref[0] * GROUPS * heads + skip_at + h]
        y = dot(mixing, xs)
        dxs = dot(mixing, g, TN)
        dscores += dot(g, xs, NT) * decay
        y_ref[:, at] = y + skip * x
        dx_ref[:, at] = dxs * step + skip * gf
        gy_ref[:, one] = jnp.sum(gf * y, axis=1, keepdims=True)
        ds_ref[:, one] = jnp.sum(x * dxs, axis=1, keepdims=True)
        gx_ref[0:1, one] = jnp.sum(jnp.sum(gf * x, axis=0, keepdims=True), axis=1, keepdims=True)
    dscores_ref[...] = jnp.where(mask, dscores, 0.0)


def inside_bc_kernel(bc0_ref, bc1_ref, *refs):
    parts, outs = refs[: 2 * GROUPS], refs[2 * GROUPS :]
    for slot, bc_ref in enumerate((bc0_ref, bc1_ref)):
        total = parts[slot * GROUPS][...]
        for i in range(1, GROUPS):
            total = total + parts[slot * GROUPS + i][...]
        ds = total.astype(BF16)
        outs[slot][:, :LANES] = dot(ds, bc_ref[:, LANES:], TN)
        outs[slot][:, LANES:] = dot(ds, bc_ref[:, :LANES])


def across_kernel(
    heads, lanes, hops, idx_ref, offs_ref, x0_ref, g0_ref, back_ref, bc0_ref, bc1_ref, xe0_ref,
    ge0_ref, xe1_ref, ge1_ref, step_ref, grow_ref, endw_ref, dec_ref, p_ref, sf_ref, ds_ref,
    y0_ref, dx0_ref, y1_ref, dx1_ref, dbc0_ref, dbc1_ref, *refs
):
    received = refs[: hops * CHUNKS]
    (
        yo_ref, dxo_ref, send_ref, dbco0_ref, dbco1_ref, u_ref, t_ref, re_ref,
        e_in, r_in, e_scr, r_scr, n_scr,
    ) = refs[hops * CHUNKS :]
    r, pos = idx_ref[0], idx_ref[1]
    width = back_ref.shape[1] // 2
    part = width // CHUNKS
    e_in[...] = jnp.zeros_like(e_in)
    r_in[...] = jnp.zeros_like(r_in)
    for k in range(hops):
        for i in range(CHUNKS):
            at = slice(i * part, (i + 1) * part)

            @pl.when(pos - 1 == k)
            def _(k=k, i=i, at=at):
                e_in[:, at] = received[k * CHUNKS + i][...]

            @pl.when(hops - 1 - pos == k)
            def _(k=k, i=i, at=at):
                r_in[:, at] = received[k * CHUNKS + i][...]

    dec_pair, dec_first, dec_second = dec_ref[0:1, :], dec_ref[1:2, :], dec_ref[2:3, :]
    entering = e_in[...].astype(F32)
    later = r_in[...].astype(F32)
    middle = dec_first * entering + sf_ref[...].astype(F32)
    leaving = dec_pair * entering + p_ref[...].astype(F32)
    earlier = dec_second * later + ds_ref[...].astype(F32)
    e_scr[r] = e_in[...]
    e_scr[1 - r] = middle.astype(BF16)
    r_scr[1 - r] = r_in[...]
    r_scr[r] = earlier.astype(BF16)
    n_scr[1 - r] = jnp.sum(later * leaving, axis=0, keepdims=True)
    n_scr[r] = jnp.sum(earlier * middle, axis=0, keepdims=True)

    u_ref[...] = jnp.zeros_like(u_ref)
    t_ref[...] = jnp.zeros_like(t_ref)
    re_ref[...] = jnp.zeros_like(re_ref)
    for slot, (bc_ref, xe_ref, ge_ref, y_ref, dx_ref, dbc_ref, dbco_ref) in enumerate(
        (
            (bc0_ref, xe0_ref, ge0_ref, y0_ref, dx0_ref, dbc0_ref, dbco0_ref),
            (bc1_ref, xe1_ref, ge1_ref, y1_ref, dx1_ref, dbc1_ref, dbco1_ref),
        )
    ):
        e_all = e_scr[slot]
        r_all = r_scr[slot]
        dbco_ref[:, :LANES] = dbc_ref[:, :LANES] + dot(xe_ref[...], r_all, NT)
        dbco_ref[:, LANES:] = dbc_ref[:, LANES:] + dot(ge_ref[...], e_all, NT)
        ce_all = dot(bc_ref[:, LANES:], e_all)
        br_all = dot(bc_ref[:, :LANES], r_all)
        for h in range(heads):
            at = slice(h * LANES, (h + 1) * LANES)
            lane = lanes[slot] + h
            one = slice(lane, lane + 1)
            ce, br = ce_all[:, at], br_all[:, at]
            y = (y_ref[:, at] + grow_ref[:, one] * ce).astype(BF16)
            dx = (dx_ref[:, at] + (step_ref[:, one] * endw_ref[:, one]) * br).astype(BF16)
            if slot == 0:
                yo_ref[:, at] = y
                dxo_ref[:, at] = dx
                x = x0_ref[:, aligned(offs_ref[0] + h * LANES, LANES)].astype(F32)
                g = g0_ref[:, aligned(offs_ref[1] + h * LANES, LANES)].astype(F32)
            else:
                send_ref[:, at] = y
                send_ref[:, width + h * LANES : width + (h + 1) * LANES] = dx
                x = back_ref[:, at].astype(F32)
                g = back_ref[:, width + h * LANES : width + (h + 1) * LANES].astype(F32)
            u_ref[:, one] = jnp.sum(g * ce, axis=1, keepdims=True)
            t_ref[:, one] = jnp.sum(x * br, axis=1, keepdims=True)
            re_ref[0:1, one] = jnp.sum(n_scr[slot][:, at], axis=1, keepdims=True)


def steps_kernel(dt_ref, bias_ref, alog_ref, step_ref, grow_ref, endw_ref, *refs):
    count = 2 * GROUPS
    gys, dss, gxs = refs[:count], refs[count : 2 * count], refs[2 * count : 3 * count]
    refs = refs[3 * count :]
    us, ts, res = refs[:GROUPS], refs[GROUPS : 2 * GROUPS], refs[2 * GROUPS : 3 * GROUPS]
    draw_ref, sums_ref = refs[3 * GROUPS :]

    def total(parts):
        value = parts[0][...]
        for a in parts[1:]:
            value = value + a[...]
        return value

    n = step_ref.shape[0]
    step = step_ref[...]
    ds = total(dss) + endw_ref[...] * total(ts)
    gy = total(gys) + grow_ref[...] * total(us)
    rate = jnp.exp(alog_ref[...])
    last = lax.broadcasted_iota(jnp.int32, (n, LANES), 0) == n - 1
    dcum = gy - step * ds + jnp.where(last, total(res)[0:1, :], 0.0)
    lower = jnp.where(triangle(n), 1.0, 0.0).astype(F32)
    dlog = dot(lower, dcum, TN, precision=HIGHEST)
    draw = (ds - rate * dlog) * jax.nn.sigmoid(dt_ref[...] + bias_ref[...])
    draw_ref[...] = draw
    sums_ref[0:1, :] = jnp.sum(draw, axis=0, keepdims=True)
    sums_ref[1:2, :] = jnp.sum(dlog * (-step * rate), axis=0, keepdims=True)
    sums_ref[2:3, :] = total(gxs)[0:1, :]
    sums_ref[3:8, :] = jnp.zeros((5, LANES), F32)


def conv_back_kernel(
    idx_ref, own_ref, ret_ref, pre_ref, ext_ref, cw_ref, heads_ref, grad_ref, message_ref, z_scr, sum_scr
):
    tokens = pre_ref.shape[0]
    taps = cw_ref.shape[0]
    pre = pre_ref[...]
    sig = jax.nn.sigmoid(pre)
    dconv = (own_ref[...] + ret_ref[...].astype(F32)) * sig * (1.0 + pre * (1.0 - sig))
    z_scr[...] = jnp.zeros_like(z_scr)
    z_scr[HALO : HALO + tokens, :] = dconv
    grad = cw_ref[0:1, :] * z_scr[taps - 1 : taps - 1 + tokens + HALO, :]
    for k in range(1, taps):
        grad = grad + cw_ref[k : k + 1, :] * z_scr[taps - 1 - k : taps - 1 - k + tokens + HALO, :]
    grad_ref[...] = grad
    first = HALO - taps + 1
    sum_scr[...] = jnp.zeros_like(sum_scr)
    for k in range(taps):
        sum_scr[k : k + 1, :] = jnp.sum(
            dconv * ext_ref[first + k : first + k + tokens, :], axis=0, keepdims=True
        )
    sum_scr[taps : taps + 1, :] = jnp.sum(dconv, axis=0, keepdims=True)
    sum_scr[8:11, aligned(idx_ref[0] * LANES, LANES)] = heads_ref[0:3, :]
    high, low = split(sum_scr[...])
    message_ref[0 : tokens + HALO, :] = grad.astype(BF16)
    message_ref[tokens + HALO : tokens + HALO + 16, :] = high
    message_ref[tokens + HALO + 16 :, :] = low


def pack_kernel(count, offs_ref, layer_ref, halo_ref, *outs):
    for k in range(count):
        at = aligned(offs_ref[k], outs[k].shape[1])
        outs[k][0:HALO, :] = halo_ref[:, at]
        outs[k][HALO:, :] = layer_ref[:, at]


def turn_kernel(count, *refs):
    out = refs[count]
    tokens = refs[0].shape[0] - HALO
    for k in range(count):
        out[:, k * tokens : (k + 1) * tokens] = refs[k][HALO:, :].T
    halos = jnp.concatenate([refs[k][0:HALO, :] for k in range(count)], 0)
    out[:, count * tokens :] = halos.T


def weight_kernel(count, size, offs_ref, left_ref, *refs):
    rights, outs, total = refs[:count], refs[count : count + size], refs[count + size]
    tokens = (left_ref.shape[1] // count) - HALO
    right = jnp.concatenate(
        [a[HALO : HALO + tokens, :] for a in rights] + [a[0:HALO, :] for a in rights], 0
    )
    total[...] = dot(left_ref[...], right)
    at = tokens + HALO
    small = jnp.zeros((16, right.shape[1]), F32)
    for a in rights:
        small += a[at : at + 16, :].astype(F32) + a[at + 16 : at + 32, :].astype(F32)
    high, low = split(small)
    chunk = outs[0].shape[0] - 32
    for k in range(size):
        outs[k][0:chunk, :] = total[pl.ds(pl.multiple_of(offs_ref[k], chunk), chunk), :].astype(BF16)
        outs[k][chunk : chunk + 16, :] = high
        outs[k][chunk + 16 :, :] = low


def reduce_kernel(count, *refs):
    total_ref, small_ref = refs[count:]
    chunk = total_ref.shape[0]
    total = refs[0][...].astype(F32)
    for k in range(1, count):
        total = total + refs[k][...].astype(F32)
    total_ref[...] = total[0:chunk].astype(BF16)
    small_ref[...] = total[chunk : chunk + 16] + total[chunk + 16 :]


def place_rows_kernel(count, offs_ref, *refs):
    out = refs[count]
    chunk = refs[0].shape[0]
    for k in range(count):
        out[pl.ds(pl.multiple_of(offs_ref[k], chunk), chunk), :] = refs[k][...].astype(F32)


def tokens_kernel(count, offs_ref, grad_ref, rim_ref, *refs):
    pieces, out = refs[:count], refs[count]
    own = grad_ref[HALO:, :]
    tail = rim_ref.shape[0]
    g = jnp.concatenate([own[:-tail], own[-tail:] + rim_ref[...]], 0).astype(BF16)
    rows = pieces[0].shape[0]
    for k in range(count):
        out[:, aligned(offs_ref[k], rows)] = dot(g, pieces[k][...], NT).astype(BF16)


def join_kernel(offs_ref, *refs):
    own_y, own_dx, back = refs[:GROUPS], refs[GROUPS : 2 * GROUPS], refs[2 * GROUPS : 3 * GROUPS]
    y_ref, dx_ref = refs[3 * GROUPS :]
    width = own_y[0].shape[1]
    for i in range(GROUPS):
        mine, others = (aligned(offs_ref[j] + i * width, width) for j in range(2))
        y_ref[:, mine] = own_y[i][...]
        dx_ref[:, mine] = own_dx[i][...]
        y_ref[:, others] = back[i][:, :width]
        dx_ref[:, others] = back[i][:, width:]


def toggled(x, axis, bits):
    size = lax.axis_size(axis)
    return lax.ppermute(x, axis, [(i, i ^ bits) for i in range(size)])


def chain(p, q, decay, axis):
    pairs = lax.axis_size(axis) // 2
    pos = lax.axis_index(axis) // 2
    received = []
    for hop in range(pairs - 1):
        value = jnp.where(pos == hop, p, q)
        if hop:
            value = decay * received[-1].astype(F32) + value.astype(F32)
        lanes = [(hop, hop + 1), (pairs - 1 - hop, pairs - 2 - hop)]
        lanes = [(2 * a + i, 2 * b + i) for a, b in lanes for i in range(2)]
        received.append(lax.ppermute(value.astype(BF16), axis, lanes))
    return received


def body(layer_in, w_bc, conv_w, conv_b, ssm_in, dt_raw, dt_bias, a_log, skip_scale, grad_out):
    ctx, fsdp = lax.axis_size("ctx"), lax.axis_size("fsdp")
    d, f = lax.axis_index("ctx").astype(jnp.int32), lax.axis_index("fsdp").astype(jnp.int32)
    r = d % 2
    layer, x, g, dt = layer_in[0], ssm_in[0], grad_out[0], dt_raw[0]
    tokens, width = x.shape
    total_heads = dt_bias.shape[0]
    heads = total_heads // 2
    half = width // 2
    hg, gw = heads // GROUPS, half // GROUPS
    state = w_bc.shape[1] // 2
    taps = conv_w.shape[0]
    rows = w_bc.shape[0]
    chunk_rows = rows // ctx
    hops = ctx // 2 - 1
    idx = jnp.stack([r, d // 2])
    own_at, other_at = r * half, (1 - r) * half
    column_offs = (jnp.arange(fsdp, dtype=jnp.int32) ^ f) * rows
    row_offs = (jnp.arange(ctx, dtype=jnp.int32) ^ d) * chunk_rows
    square = shape((tokens, LANES), F32)

    def mine(a):
        n = a.shape[-1] // 2
        return jnp.where(r == 0, a[..., :n], a[..., n:])

    halo = lax.ppermute(layer[tokens - HALO :], "ctx", [(i, i + 1) for i in range(ctx - 1)])
    pieces = {0: w_bc}
    bit = fsdp // 2
    while bit:
        for k in list(pieces):
            pieces[k | bit] = toggled(pieces[k], "fsdp", bit)
        bit //= 2
    pieces = [pieces[k] for k in range(fsdp)]
    n = dt.shape[1] // 2
    dt_recv = toggled(jnp.where(r == 0, dt[:, n:], dt[:, :n]), "ctx", 1)
    swaps = pl.pallas_call(
        swap_kernel,
        out_shape=[shape((tokens, 2 * gw), BF16)] * GROUPS,
        in_specs=[pl.BlockSpec(memory_space=pltpu.SMEM)] + [pl.BlockSpec(memory_space=pl.ANY)] * 2,
        out_specs=[pl.BlockSpec(memory_space=pltpu.VMEM)] * GROUPS,
        scratch_shapes=[pltpu.SemaphoreType.DMA((2 * GROUPS,))],
        compiler_params=pltpu.CompilerParams(vmem_limit_bytes=LIMIT),
        name="swap",
    )(other_at[None], x, g)
    swapped = [toggled(a, "ctx", 1) for a in swaps]

    def lanes_of(a):
        return jnp.pad(a, ((0, 0), (0, LANES - a.shape[1])))

    def twice(a):
        m = mine(a)[None, :]
        return lanes_of(jnp.concatenate([m, m], 1))

    dt2 = lanes_of(jnp.concatenate([mine(dt), dt_recv], 1))
    bias2, alog2 = twice(dt_bias), twice(a_log)
    step, cum, cumt, grow, endw = call(vectors_kernel, "vectors", [square] * 5, (), dt2, bias2, alog2)

    def source(slot, i):
        if slot == 0:
            at = own_at + i * gw
            return jnp.stack([at, at]), x, g
        return jnp.array([0, gw], jnp.int32), swapped[i], swapped[i]

    flat = shape((tokens, gw), BF16)
    scaled = {}
    for slot in range(2):
        for i in range(GROUPS):
            offs, xa, ga = source(slot, i)
            scaled[slot, i] = call(
                functools.partial(scale_kernel, hg, slot * heads + i * hg), "scale", [flat, flat],
                (offs,), xa, ga, step, grow, endw,
            )

    ext, pre, bc = call(
        functools.partial(project_kernel, fsdp), "project",
        [
            shape((tokens + HALO, 2 * state), F32),
            shape((tokens, 2 * state), F32),
            shape((tokens, 2 * state), BF16),
        ],
        (column_offs,), layer, halo, *pieces, conv_w, conv_b[None, :],
    )
    bcs = [bc, toggled(bc, "ctx", 1)]

    states, received = [], []
    for i in range(GROUPS):
        lanes = (i * hg, heads + i * hg)
        wide = shape((state, gw), BF16)
        p, q, s_first, d_second, decays = call(
            functools.partial(states_kernel, hg, lanes), "states",
            [wide] * 4 + [shape((8, gw), F32)],
            (idx,), *bcs, *scaled[0, i], *scaled[1, i], grow,
            scratch=[pltpu.VMEM((2, state, gw), F32)] * 2 + [pltpu.VMEM((2, 1, gw), F32)],
        )
        states.append((decays, p, s_first, d_second))
        part = gw // CHUNKS
        cut = [slice(k * part, (k + 1) * part) for k in range(CHUNKS)]
        links = [chain(p[:, a], q[:, a], decays[0:1, a], "ctx") for a in cut]
        received.append([links[k][hop] for hop in range(hops) for k in range(CHUNKS)])

    inside = {}
    for slot in range(2):
        for i in range(GROUPS):
            offs, xa, ga = source(slot, i)
            inside[slot, i] = call(
                functools.partial(inside_kernel, hg, slot * heads + i * hg, i * hg), "inside",
                [shape((tokens, gw), F32)] * 2 + [shape((tokens, tokens), F32), square, square]
                + [shape((8, LANES), F32)],
                (idx, offs, skip_scale), xa, ga, bcs[slot], step, cum, cumt,
            )
    order = [(slot, i) for slot in range(2) for i in range(GROUPS)]
    dbcs = call(
        inside_bc_kernel, "inside_bc", [shape((tokens, 2 * state), F32)] * 2, (),
        *bcs, *[inside[key][2] for key in order],
    )

    late_layer, late_halo, _ = lax.optimization_barrier((layer, halo, bc))
    packs = call(
        functools.partial(pack_kernel, fsdp), "pack", [shape((tokens + HALO, rows), BF16)] * fsdp,
        (column_offs,), late_layer, late_halo,
    )
    lefts = [packs[0]] + [toggled(packs[k], "fsdp", k) for k in range(1, fsdp)]
    left = call(
        functools.partial(turn_kernel, fsdp), "turn", shape((rows, fsdp * (tokens + HALO)), BF16),
        (), *lefts,
    )

    own_y, own_dx, sends, us, ts, res = [], [], [], [], [], []
    for i in range(GROUPS):
        offs, xa, ga = source(0, i)
        lanes = (i * hg, heads + i * hg)
        y, dx, send, *dbcs, u, t, re = call(
            functools.partial(across_kernel, hg, lanes, hops), "across",
            [flat, flat, shape((tokens, 2 * gw), BF16)] + [shape((tokens, 2 * state), F32)] * 2
            + [square, square, shape((8, LANES), F32)],
            (idx, offs), xa, ga, swapped[i], *bcs, *scaled[0, i], *scaled[1, i], step, grow, endw,
            *states[i], *inside[0, i][:2], *inside[1, i][:2], *dbcs, *received[i],
            scratch=[pltpu.VMEM((state, gw), BF16)] * 2 + [pltpu.VMEM((2, state, gw), BF16)] * 2
            + [pltpu.VMEM((2, 1, gw), F32)],
        )
        own_y.append(y)
        own_dx.append(dx)
        sends.append(send)
        us.append(u)
        ts.append(t)
        res.append(re)

    dbc_ret = toggled(dbcs[1].astype(BF16), "ctx", 1)
    draw, head_sums = call(
        steps_kernel, "steps", [square, shape((8, LANES), F32)], (), dt2, bias2, alog2, step, grow,
        endw, *[inside[key][j] for j in (3, 4, 5) for key in order], *us, *ts, *res,
    )
    grad, message = call(
        conv_back_kernel, "conv_back",
        [
            shape((tokens + HALO, 2 * state), F32),
            shape((tokens + HALO + 32, 2 * state), BF16),
        ],
        (idx,), dbcs[0], dbc_ret, pre, ext, conv_w, head_sums,
        scratch=[
            pltpu.VMEM((tokens + 2 * HALO, 2 * state), F32),
            pltpu.VMEM((16, 2 * state), F32),
        ],
    )

    rights = [message] + [toggled(message, "fsdp", k) for k in range(1, fsdp)]
    terms = call(
        functools.partial(weight_kernel, fsdp, ctx), "weight",
        [shape((chunk_rows + 32, 2 * state), BF16)] * ctx,
        (row_offs,), left, *rights,
        scratch=[pltpu.VMEM((rows, 2 * state), F32)],
    )
    arrived = [terms[0]] + [toggled(terms[k], "ctx", k) for k in range(1, ctx)]
    total, small = call(
        functools.partial(reduce_kernel, ctx), "reduce",
        [shape((chunk_rows, 2 * state), BF16), shape((16, 2 * state), F32)], (), *arrived,
    )
    everyones = [total] + [toggled(total, "ctx", k) for k in range(1, ctx)]
    grad_weight = call(
        functools.partial(place_rows_kernel, ctx), "place_rows", shape((rows, 2 * state), F32),
        (row_offs,), *everyones,
    )
    folded = small[8:11].reshape(3, 2, LANES)
    per_head = (folded[:, :, :heads] + folded[:, :, heads : 2 * heads]).reshape(3, total_heads)

    rim = lax.ppermute(grad[HALO - 8 : HALO], "ctx", [(i + 1, i) for i in range(ctx - 1)])
    grad_tokens = call(
        functools.partial(tokens_kernel, fsdp), "grad_tokens", shape((tokens, fsdp * rows), BF16),
        (column_offs,), grad, rim, *pieces,
    )
    backs = [toggled(a, "ctx", 1) for a in sends]
    ssm_out, grad_values = call(
        join_kernel, "join", [shape((tokens, width), BF16)] * 2, (jnp.stack([own_at, other_at]),),
        *own_y, *own_dx, *backs,
    )
    own_raw, back_raw = draw[:, :heads], toggled(draw[:, heads : 2 * heads], "ctx", 1)
    grad_raw = jnp.where(
        r == 0,
        jnp.concatenate([own_raw, back_raw], 1),
        jnp.concatenate([back_raw, own_raw], 1),
    )
    return (
        ssm_out[None],
        grad_values[None],
        grad_tokens[None],
        grad_raw[None],
        grad_weight,
        small[:taps],
        small[taps],
        per_head[0],
        per_head[1],
        per_head[2],
    )


def solution(mesh):
    tokens = P("fsdp", "ctx", None)
    in_specs = (tokens, P("fsdp", None), P(), P(), tokens, tokens, P(), P(), P(), tokens)
    out_specs = (tokens, tokens, tokens, tokens, P("fsdp", None), P(), P(), P(), P(), P())
    return jax.shard_map(body, mesh=mesh, in_specs=in_specs, out_specs=out_specs, check_vma=False)
```

time: 182 us -> 175 us (0.962)
  waiting for transfers between devices: 71.3 us -> 32.7 us
  local copies, waits for them, and re-layouts: 15.1 us -> 29.3 us
  Pallas kernels: 28 us -> 37.2 us
  starting transfers between devices: 57.7 us -> 62.8 us
    ppermute x13 -> x7, waiting for transfers between devices: 35.8 us -> 5.97 us  [the longest x1 5.95 us: body(): lax.ppermute(layer[tokens - HALO:], 'ctx', [(i, i + 1) for i in range(ctx...]
    ppermute x36 -> x31, waiting for transfers between devices: 31.6 us -> 12.9 us  [toggled(): return lax.ppermute(x, axis, [(i, i ^ bits) for i in range(size)])]
    ppermute x1, waiting for transfers between devices: 3.99 us -> 13.9 us  [body(): lax.ppermute(grad[HALO - 8:HALO], 'ctx', [(i + 1, i) for i in range(ctx -...]
    pallas_call x9 -> x25, Pallas kernels: 28 us -> 37.2 us  [the longest x24 36.2 us: call(): pl.pallas_call(kernel, out_shape=outs, in_specs=[pl.BlockSpec(memory_spac...]
    unnamed x72 -> x202, local copies, waits for them, and re-layouts: 12.1 us -> 21.1 us
    ppermute x36 -> x31, starting transfers between devices: 39.9 us -> 47.5 us  [toggled(): return lax.ppermute(x, axis, [(i, i ^ bits) for i in range(size)])]
    convert_element_type x6 -> x5, other arithmetic: 1.78 us -> 6.16 us  [the longest x4 6.15 us: chain(): received.append(lax.ppermute(value.astype(BF16), axis, lanes))]
    select_n x7 -> x4, other arithmetic: 6.04 us -> 2.92 us  [the longest x2 1.53 us: chain(): value = jnp.where(pos == hop, p, q)]
  transfers between devices with their start and end apart: 50 -> 39, of which waited for: 17 -> 11; matrix products, arithmetic and copies ran while one was open for 5% -> 10% of each run, Pallas kernels for 14% -> 19%
where the time goes in v2:
time: 175 us; the launch traced here: 174 us
  starting transfers between devices  62.8 us (36%)
  Pallas kernels  37.2 us (21%)
  waiting for transfers between devices  32.7 us (19%)
  local copies, waits for them, and re-layouts  29.3 us (17%)
  other arithmetic  9.7 us (6%)
  between operations  1.84 us (1%)
    ppermute x31, starting transfers between devices, toggled(): return lax.ppermute(x, axis, [(i, i ^ bits) for i in range(size)])  47.5 us
    pallas_call x24, Pallas kernels, call(): pl.pallas_call(kernel, out_shape=outs, in_specs=[pl.BlockSpec(memory_spac...  36.2 us
    unnamed x202, local copies, waits for them, and re-layouts  21.1 us
    ppermute x1, waiting for transfers between devices, body(): lax.ppermute(grad[HALO - 8:HALO], 'ctx', [(i + 1, i) for i in range(ctx -...  13.9 us
    ppermute x31, waiting for transfers between devices, toggled(): return lax.ppermute(x, axis, [(i, i ^ bits) for i in range(size)])  12.9 us
    ppermute x6, starting transfers between devices, chain(): received.append(lax.ppermute(value.astype(BF16), axis, lanes))  11.6 us
    convert_element_type x4, other arithmetic, chain(): received.append(lax.ppermute(value.astype(BF16), axis, lanes))  6.15 us
    ppermute x1, waiting for transfers between devices, body(): lax.ppermute(layer[tokens - HALO:], 'ctx', [(i, i + 1) for i in range(ctx...  5.95 us
  transfers between devices with their start and end apart: 39, of which 11 were waited for; matrix products, arithmetic and copies ran while one was open for 10% of the time, Pallas kernels for 19%

profile of v2, /device:TPU:0, one launch (start us, length us, event | category | flops | bytes accessed | tf_op | source)
XLA Modules:
  0.0 173.7 jit_solution(12291841866568268142)
XLA Ops:
  1.2 2.6 %collective-permute-start.3 = (bf16[1024,256]{1,0:T(8,128)(2,1)}, bf16[1024,256]{1,0:T(8,128)(2,1)S(1)}, u32[]{:S(2)}, u32[]{:S(2)}) collective-permute-start(bf16[1024,256]{1,0:T(8,128)(2,1)} %refs_0_.3), channel_id=1, source_target_pairs={{0,2},{1,3},{2,0},{3,1},{4,6},{5,7},{6,4},{7,5},{8,10},{9,11},{10,... | collective-permute-start | bytes 1572872 | tf_op jit(solution)/shard_map/ppermute | solution.py:417
  9.8 2.4 %collective-permute-start.1 = (bf16[16,4096]{1,0:T(8,128)(2,1)S(1)}, bf16[16,4096]{1,0:T(8,128)(2,1)S(1)}, u32[]{:S(2)}, u32[]{:S(2)}) collective-permute-start(bf16[16,4096]{1,0:T(8,128)(2,1)S(1)} %slice_bitcast_fusion), channel_id=1, source_target_pairs={{0,4},{4,8},{8,12},{12,16},{16,20},{20,24},{24,28},{1,5},{5,9},{9,... | collective-permute-start | bytes 393224 | tf_op jit(solution)/shard_map/ppermute | solution.py:459
  12.3 2.6 %collective-permute-start.6 = (f32[128,16]{0,1:T(8,128)S(1)}, f32[128,16]{0,1:T(8,128)S(1)}, u32[]{:S(2)}, u32[]{:S(2)}) collective-permute-start(f32[128,16]{0,1:T(8,128)S(1)} %get-tuple-element.207), channel_id=1, source_target_pairs={{0,4},{4,0},{8,12},{12,8},{16,20},{20,16},{24,28},{28,24},{1,5},{5... | collective-permute-start | bytes 24584 | tf_op jit(solution)/shard_map/ppermute | solution.py:417
  17.6 6.0 %collective-permute-done.1.halo_ref = bf16[16,4096]{1,0:T(8,128)(2,1)S(1)} collective-permute-done((bf16[16,4096]{1,0:T(8,128)(2,1)S(1)}, bf16[16,4096]{1,0:T(8,128)(2,1)S(1)}, u32[]{:S(2)}, u32[]{:S(2)}) %collective-permute-start.1) | collective-permute-done | bytes 131104 | tf_op jit(solution)/shard_map/ppermute | solution.py:459
  23.5 2.5 %collective-permute-start.7 = (bf16[128,2048]{1,0:T(8,128)(2,1)}, bf16[128,2048]{1,0:T(8,128)(2,1)S(1)}, u32[]{:S(2)}, u32[]{:S(2)}) collective-permute-start(bf16[128,2048]{1,0:T(8,128)(2,1)} %get-tuple-element.124), channel_id=1, source_target_pairs={{0,4},{4,0},{8,12},{12,8},{16,20},{20,16},{24,28},{28,24},{1,5},{5... | collective-permute-start | bytes 1572872 | tf_op jit(solution)/shard_map/ppermute | solution.py:417
  43.3 4.2 %collective-permute-start.8 = (bf16[128,1024]{1,0:T(8,128)(2,1)}, bf16[128,1024]{1,0:T(8,128)(2,1)}, u32[]{:S(2)}, u32[]{:S(2)}) collective-permute-start(bf16[128,1024]{1,0:T(8,128)(2,1)} %broadcast_select_fusion.1), channel_id=1, source_target_pairs={{0,8},{4,12},{24,16},{28,20},{1,9},{5,13},{25,17},{29,21},{2,10},{... | collective-permute-start | bytes 786440 | tf_op jit(solution)/shard_map/ppermute | solution.py:430
  53.0 2.0 %collective-permute-start.11 = (bf16[128,1024]{1,0:T(8,128)(2,1)}, bf16[128,1024]{1,0:T(8,128)(2,1)}, u32[]{:S(2)}, u32[]{:S(2)}) collective-permute-start(bf16[128,1024]{1,0:T(8,128)(2,1)} %broadcast_select_fusion), channel_id=1, source_target_pairs={{0,8},{4,12},{24,16},{28,20},{1,9},{5,13},{25,17},{29,21},{2,10},{... | collective-permute-start | bytes 786440 | tf_op jit(solution)/shard_map/ppermute | solution.py:430
  71.5 2.3 %inside.4 = (f32[128,1024]{1,0:T(8,128)S(1)}, f32[128,1024]{1,0:T(8,128)S(1)}, f32[128,128]{1,0:T(8,128)S(1)}, f32[128,128]{1,0:T(8,128)S(1)}, f32[128,128]{1,0:T(8,128)S(1)}, /*index=5*/f32[8,128]{1,0:T(8,128)S(1)}) custom-call(s32[2]{0:T(128)S(1)} %pad_add_fusion.1.idx_ref, s32[2]{0:T(128)S(1)} %pad_add_fusion.2.offs_ref, f32[32]{0:T(128)S(1)} %copy-done.82, ...), custom_call_target="tpu_custom_call" | custom-call | bytes 3608576 | tf_op jit(solution)/shard_map/inside/pallas_call | solution.py:36
  73.8 2.3 %inside.6 = (f32[128,1024]{1,0:T(8,128)S(1)}, f32[128,1024]{1,0:T(8,128)S(1)}, f32[128,128]{1,0:T(8,128)S(1)}, f32[128,128]{1,0:T(8,128)S(1)}, f32[128,128]{1,0:T(8,128)S(1)}, /*index=5*/f32[8,128]{1,0:T(8,128)S(1)}) custom-call(s32[2]{0:T(128)S(1)} %pad_add_fusion.1.idx_ref, s32[2]{0:T(128)S(1)} %copy-done.85, f32[32]{0:T(128)S(1)} %copy-done.82, ...), custom_call_target="tpu_custom_call" | custom-call | bytes 3608576 | tf_op jit(solution)/shard_map/inside/pallas_call | solution.py:36
  76.2 2.3 %inside.5 = (f32[128,1024]{1,0:T(8,128)S(1)}, f32[128,1024]{1,0:T(8,128)S(1)}, f32[128,128]{1,0:T(8,128)S(1)}, f32[128,128]{1,0:T(8,128)S(1)}, f32[128,128]{1,0:T(8,128)S(1)}, /*index=5*/f32[8,128]{1,0:T(8,128)S(1)}) custom-call(s32[2]{0:T(128)S(1)} %pad_add_fusion.1.idx_ref, s32[2]{0:T(128)S(1)} %iota_multiply_fusion.offs_ref, f32[32]{0:T(128)S(1)} %copy-done.82, ...), custom_call_target="tpu_custom_call" | custom-call | bytes 2560000 | tf_op jit(solution)/shard_map/inside/pallas_call | solution.py:36
  78.5 2.3 %inside.7 = (f32[128,1024]{1,0:T(8,128)S(1)}, f32[128,1024]{1,0:T(8,128)S(1)}, f32[128,128]{1,0:T(8,128)S(1)}, f32[128,128]{1,0:T(8,128)S(1)}, f32[128,128]{1,0:T(8,128)S(1)}, /*index=5*/f32[8,128]{1,0:T(8,128)S(1)}) custom-call(s32[2]{0:T(128)S(1)} %pad_add_fusion.1.idx_ref, s32[2]{0:T(128)S(1)} %iota_multiply_fusion.offs_ref, f32[32]{0:T(128)S(1)} %copy-done.82, ...), custom_call_target="tpu_custom_call" | custom-call | bytes 2560000 | tf_op jit(solution)/shard_map/inside/pallas_call | solution.py:36
  81.2 3.8 %across.2 = (bf16[128,1024]{1,0:T(8,128)(2,1)S(1)}, bf16[128,1024]{1,0:T(8,128)(2,1)S(1)}, bf16[128,2048]{1,0:T(8,128)(2,1)S(1)}, f32[128,256]{1,0:T(8,128)S(1)}...) custom-call(s32[2]{0:T(128)S(1)} %pad_add_fusion.1.idx_ref, ...), custom_call_target="tpu_custom_call" | custom-call | bytes 9408512 | tf_op jit(solution)/shard_map/across/pallas_call | solution.py:36
  86.5 3.6 %across.3 = (bf16[128,1024]{1,0:T(8,128)(2,1)S(1)}, bf16[128,1024]{1,0:T(8,128)(2,1)S(1)}, bf16[128,2048]{1,0:T(8,128)(2,1)S(1)}, f32[128,256]{1,0:T(8,128)S(1)}...) custom-call(s32[2]{0:T(128)S(1)} %pad_add_fusion.1.idx_ref, ...), custom_call_target="tpu_custom_call" | custom-call | bytes 9408512 | tf_op jit(solution)/shard_map/across/pallas_call | solution.py:36
  92.0 2.7 %collective-permute-done.16.ret_ref = bf16[128,256]{1,0:T(8,128)(2,1)S(1)} collective-permute-done((bf16[128,256]{1,0:T(8,128)(2,1)S(1)}, bf16[128,256]{1,0:T(8,128)(2,1)S(1)}, u32[]{:S(2)}, u32[]{:S(2)}) %collective-permute-start.16) | collective-permute-done | bytes 65568 | tf_op jit(solution)/shard_map/ppermute | solution.py:417
  97.9 3.1 %collective-permute-done.23.refs_2_ = bf16[176,256]{1,0:T(8,128)(2,1)S(1)} collective-permute-done((bf16[176,256]{1,0:T(8,128)(2,1)S(1)}, bf16[176,256]{1,0:T(8,128)(2,1)S(1)}, u32[]{:S(2)}, u32[]{:S(2)}) %collective-permute-start.23) | collective-permute-done | bytes 90144 | tf_op jit(solution)/shard_map/ppermute | solution.py:417
  105.3 6.2 %collective-permute-start.26 = (bf16[160,256]{1,0:T(8,128)(2,1)S(1)}, bf16[160,256]{1,0:T(8,128)(2,1)S(1)}, u32[]{:S(2)}, u32[]{:S(2)}) collective-permute-start(bf16[160,256]{1,0:T(8,128)(2,1)S(1)} %get-tuple-element.186), channel_id=1, source_target_pairs={{0,8},{4,12},{8,0},{12,4},{16,24},{20,28},{24,16},{28,20},{1,9},{5... | collective-permute-start | bytes 245768 | tf_op jit(solution)/shard_map/ppermute | solution.py:417
  113.0 3.0 %collective-permute-start.28 = (bf16[160,256]{1,0:T(8,128)(2,1)S(1)}, bf16[160,256]{1,0:T(8,128)(2,1)S(1)}, u32[]{:S(2)}, u32[]{:S(2)}) collective-permute-start(bf16[160,256]{1,0:T(8,128)(2,1)S(1)} %get-tuple-element.188), channel_id=1, source_target_pairs={{0,16},{4,20},{8,24},{12,28},{16,0},{20,4},{24,8},{28,12},{1,17},{... | collective-permute-start | bytes 245768 | tf_op jit(solution)/shard_map/ppermute | solution.py:417
  116.4 2.6 %collective-permute-start.29 = (bf16[160,256]{1,0:T(8,128)(2,1)}, bf16[160,256]{1,0:T(8,128)(2,1)}, u32[]{:S(2)}, u32[]{:S(2)}) collective-permute-start(bf16[160,256]{1,0:T(8,128)(2,1)} %get-tuple-element.189), channel_id=1, source_target_pairs={{0,20},{4,16},{8,28},{12,24},{16,4},{20,0},{24,12},{28,8},{1,21},{... | collective-permute-start | bytes 245768 | tf_op jit(solution)/shard_map/ppermute | solution.py:417
  132.1 2.5 %collective-permute-start.32 = (bf16[128,256]{1,0:T(8,128)(2,1)}, bf16[128,256]{1,0:T(8,128)(2,1)S(1)}, u32[]{:S(2)}, u32[]{:S(2)}) collective-permute-start(bf16[128,256]{1,0:T(8,128)(2,1)} %get-tuple-element.192.refs_0_), channel_id=1, source_target_pairs={{0,4},{4,0},{8,12},{12,8},{16,20},{20,16},{24,28},{28,24},{1,5},{5... | collective-permute-start | bytes 196616 | tf_op jit(solution)/shard_map/ppermute | solution.py:417
  136.0 13.9 %collective-permute-done.17.rim_ref = f32[8,256]{1,0:T(8,128)S(1)} collective-permute-done((f32[8,256]{1,0:T(8,128)S(1)}, f32[8,256]{1,0:T(8,128)S(1)}, u32[]{:S(2)}, u32[]{:S(2)}) %collective-permute-start.17) | collective-permute-done | bytes 8224 | tf_op jit(solution)/shard_map/ppermute | solution.py:619
  149.9 2.3 %grad_tokens.1 = bf16[128,4096]{1,0:T(8,128)(2,1)} custom-call(s32[4]{0:T(128)S(1)} %copy-done.88, f32[144,256]{1,0:T(8,128)S(1)} %get-tuple-element.175.grad_ref, f32[8,256]{1,0:T(8,128)S(1)} %collective-permute-done.17.rim_ref, bf16[1024,256]{1,0:T(8,128)(2,1)S(1)} %copy-done.19, bf16[1024,256]{1,0:T(8,128)(2,1)S(1)} %copy-done.22, ...), custom_call_target="tpu_custom_call" | custom-call | bytes 3301376 | tf_op jit(solution)/shard_map/grad_tokens/pallas_call | solution.py:36
  154.9 2.6 %collective-permute-done.33.refs_2_ = bf16[128,256]{1,0:T(8,128)(2,1)S(1)} collective-permute-done((bf16[128,256]{1,0:T(8,128)(2,1)}, bf16[128,256]{1,0:T(8,128)(2,1)S(1)}, u32[]{:S(2)}, u32[]{:S(2)}) %collective-permute-start.33) | collective-permute-done | bytes 65568 | tf_op jit(solution)/shard_map/ppermute | solution.py:417
  160.9 4.5 %collective-permute-start.38 = (bf16[128,256]{1,0:T(8,128)(2,1)}, bf16[128,256]{1,0:T(8,128)(2,1)S(1)}, u32[]{:S(2)}, u32[]{:S(2)}) collective-permute-start(bf16[128,256]{1,0:T(8,128)(2,1)} %get-tuple-element.192.refs_0_), channel_id=1, source_target_pairs={{0,28},{4,24},{8,20},{12,16},{16,12},{20,8},{24,4},{28,0},{1,29},{... | collective-permute-start | bytes 196616 | tf_op jit(solution)/shard_map/ppermute | solution.py:417
  171.7 2.0 %join.1 = (bf16[128,4096]{1,0:T(8,128)(2,1)}, bf16[128,4096]{1,0:T(8,128)(2,1)}) custom-call(s32[2]{0:T(128)S(1)} %pad_add_fusion.offs_ref, bf16[128,1024]{1,0:T(8,128)(2,1)S(1)} %copy-done.54, bf16[128,1024]{1,0:T(8,128)(2,1)S(1)} %copy-done.58, bf16[128,1024]{1,0:T(8,128)(2,1)S(1)} %copy-done.56, bf16[128,1024]{1,0:T(8,128)(2,1)S(1)} %copy-done.60, ...), custom_call_target="tpu_custom_call" | custom-call | bytes 4194304 | tf_op jit(solution)/shard_map/join/pallas_call | solution.py:36
  (319 shorter events, 87.7 us)
Async XLA Ops:
  0.7 25.4 %collective-permute-start.2 = (bf16[1024,256]{1,0:T(8,128)(2,1)}, bf16[1024,256]{1,0:T(8,128)(2,1)S(1)}, u32[]{:S(2)}, u32[]{:S(2)}) collective-permute-start(bf16[1024,256]{1,0:T(8,128)(2,1)} %refs_0_.3), channel_id=1, source_target_pairs={{0,1},{1,0},{2,3},{3,2},{4,5},{5,4},{6,7},{7,6},{8,9},{9,8},{10,11... | collective-permute-start | bytes 1572872 | tf_op jit(solution)/shard_map/ppermute | solution.py:417
  1.2 15.3 %collective-permute-start.3 = (bf16[1024,256]{1,0:T(8,128)(2,1)}, bf16[1024,256]{1,0:T(8,128)(2,1)S(1)}, u32[]{:S(2)}, u32[]{:S(2)}) collective-permute-start(bf16[1024,256]{1,0:T(8,128)(2,1)} %refs_0_.3), channel_id=1, source_target_pairs={{0,2},{1,3},{2,0},{3,1},{4,6},{5,7},{6,4},{7,5},{8,10},{9,11},{10,... | collective-permute-start | bytes 1572872 | tf_op jit(solution)/shard_map/ppermute | solution.py:417
  7.3 31.7 %collective-permute-start = (bf16[128,2048]{1,0:T(8,128)(2,1)}, bf16[128,2048]{1,0:T(8,128)(2,1)S(1)}, u32[]{:S(2)}, u32[]{:S(2)}) collective-permute-start(bf16[128,2048]{1,0:T(8,128)(2,1)} %get-tuple-element.102), channel_id=1, source_target_pairs={{0,4},{4,0},{8,12},{12,8},{16,20},{20,16},{24,28},{28,24},{1,5},{5... | collective-permute-start | bytes 1572872 | tf_op jit(solution)/shard_map/ppermute | solution.py:417
  9.8 13.7 %collective-permute-start.1 = (bf16[16,4096]{1,0:T(8,128)(2,1)S(1)}, bf16[16,4096]{1,0:T(8,128)(2,1)S(1)}, u32[]{:S(2)}, u32[]{:S(2)}) collective-permute-start(bf16[16,4096]{1,0:T(8,128)(2,1)S(1)} %slice_bitcast_fusion), channel_id=1, source_target_pairs={{0,4},{4,8},{8,12},{12,16},{16,20},{20,24},{24,28},{1,5},{5,9},{9,... | collective-permute-start | bytes 393224 | tf_op jit(solution)/shard_map/ppermute | solution.py:459
  12.3 24.1 %collective-permute-start.6 = (f32[128,16]{0,1:T(8,128)S(1)}, f32[128,16]{0,1:T(8,128)S(1)}, u32[]{:S(2)}, u32[]{:S(2)}) collective-permute-start(f32[128,16]{0,1:T(8,128)S(1)} %get-tuple-element.207), channel_id=1, source_target_pairs={{0,4},{4,0},{8,12},{12,8},{16,20},{20,16},{24,28},{28,24},{1,5},{5... | collective-permute-start | bytes 24584 | tf_op jit(solution)/shard_map/ppermute | solution.py:417
  16.5 10.3 %collective-permute-start.4 = (bf16[1024,256]{1,0:T(8,128)(2,1)S(1)}, bf16[1024,256]{1,0:T(8,128)(2,1)S(1)}, u32[]{:S(2)}, u32[]{:S(2)}) collective-permute-start(bf16[1024,256]{1,0:T(8,128)(2,1)S(1)} %collective-permute-done.3.refs_2_), channel_id=1, source_target_pairs={{0,1},{1,0},{2,3},{3,2},{4,5},{5,4},{6,7},{7,6},{8,9},{9,8},{10,11... | collective-permute-start | bytes 1572872 | tf_op jit(solution)/shard_map/ppermute | solution.py:417
  23.5 25.0 %collective-permute-start.7 = (bf16[128,2048]{1,0:T(8,128)(2,1)}, bf16[128,2048]{1,0:T(8,128)(2,1)S(1)}, u32[]{:S(2)}, u32[]{:S(2)}) collective-permute-start(bf16[128,2048]{1,0:T(8,128)(2,1)} %get-tuple-element.124), channel_id=1, source_target_pairs={{0,4},{4,0},{8,12},{12,8},{16,20},{20,16},{24,28},{28,24},{1,5},{5... | collective-permute-start | bytes 1572872 | tf_op jit(solution)/shard_map/ppermute | solution.py:417
  43.3 13.3 %collective-permute-start.8 = (bf16[128,1024]{1,0:T(8,128)(2,1)}, bf16[128,1024]{1,0:T(8,128)(2,1)}, u32[]{:S(2)}, u32[]{:S(2)}) collective-permute-start(bf16[128,1024]{1,0:T(8,128)(2,1)} %broadcast_select_fusion.1), channel_id=1, source_target_pairs={{0,8},{4,12},{24,16},{28,20},{1,9},{5,13},{25,17},{29,21},{2,10},{... | collective-permute-start | bytes 786440 | tf_op jit(solution)/shard_map/ppermute | solution.py:430
  64.3 16.6 %collective-permute-start.10 = (bf16[128,1024]{1,0:T(8,128)(2,1)S(1)}, bf16[128,1024]{1,0:T(8,128)(2,1)S(1)}, u32[]{:S(2)}, u32[]{:S(2)}) collective-permute-start(bf16[128,1024]{1,0:T(8,128)(2,1)S(1)} %add_convert_fusion.2), channel_id=1, source_target_pairs={{16,24},{20,28},{8,0},{12,4},{17,25},{21,29},{9,1},{13,5},{18,26},... | collective-permute-start | bytes 786440 | tf_op jit(solution)/shard_map/ppermute | solution.py:430
  66.9 19.5 %collective-permute-start.13 = (bf16[128,1024]{1,0:T(8,128)(2,1)S(1)}, bf16[128,1024]{1,0:T(8,128)(2,1)S(1)}, u32[]{:S(2)}, u32[]{:S(2)}) collective-permute-start(bf16[128,1024]{1,0:T(8,128)(2,1)S(1)} %add_convert_fusion), channel_id=1, source_target_pairs={{16,24},{20,28},{8,0},{12,4},{17,25},{21,29},{9,1},{13,5},{18,26},... | collective-permute-start | bytes 786440 | tf_op jit(solution)/shard_map/ppermute | solution.py:430
  69.6 26.5 %collective-permute-start.19 = (bf16[144,1024]{1,0:T(8,128)(2,1)S(1)}, bf16[144,1024]{1,0:T(8,128)(2,1)S(1)}, u32[]{:S(2)}, u32[]{:S(2)}) collective-permute-start(bf16[144,1024]{1,0:T(8,128)(2,1)S(1)} %get-tuple-element.180), channel_id=1, source_target_pairs={{0,1},{1,0},{2,3},{3,2},{4,5},{5,4},{6,7},{7,6},{8,9},{9,8},{10,11... | collective-permute-start | bytes 884744 | tf_op jit(solution)/shard_map/ppermute | solution.py:417
  69.7 27.7 %collective-permute-start.20 = (bf16[144,1024]{1,0:T(8,128)(2,1)S(1)}, bf16[144,1024]{1,0:T(8,128)(2,1)S(1)}, u32[]{:S(2)}, u32[]{:S(2)}) collective-permute-start(bf16[144,1024]{1,0:T(8,128)(2,1)S(1)} %get-tuple-element.181), channel_id=1, source_target_pairs={{0,2},{1,3},{2,0},{3,1},{4,6},{5,7},{6,4},{7,5},{8,10},{9,11},{10,... | collective-permute-start | bytes 884744 | tf_op jit(solution)/shard_map/ppermute | solution.py:417
  70.2 27.2 %collective-permute-start.21 = (bf16[144,1024]{1,0:T(8,128)(2,1)S(1)}, bf16[144,1024]{1,0:T(8,128)(2,1)S(1)}, u32[]{:S(2)}, u32[]{:S(2)}) collective-permute-start(bf16[144,1024]{1,0:T(8,128)(2,1)S(1)} %get-tuple-element.182), channel_id=1, source_target_pairs={{0,3},{1,2},{2,1},{3,0},{4,7},{5,6},{6,5},{7,4},{8,11},{9,10},{10,... | collective-permute-start | bytes 884744 | tf_op jit(solution)/shard_map/ppermute | solution.py:417
  103.9 15.2 %collective-permute-start.25 = (bf16[160,256]{1,0:T(8,128)(2,1)S(1)}, bf16[160,256]{1,0:T(8,128)(2,1)S(1)}, u32[]{:S(2)}, u32[]{:S(2)}) collective-permute-start(bf16[160,256]{1,0:T(8,128)(2,1)S(1)} %get-tuple-element.185), channel_id=1, source_target_pairs={{0,4},{4,0},{8,12},{12,8},{16,20},{20,16},{24,28},{28,24},{1,5},{5... | collective-permute-start | bytes 245768 | tf_op jit(solution)/shard_map/ppermute | solution.py:417
  105.3 15.7 %collective-permute-start.26 = (bf16[160,256]{1,0:T(8,128)(2,1)S(1)}, bf16[160,256]{1,0:T(8,128)(2,1)S(1)}, u32[]{:S(2)}, u32[]{:S(2)}) collective-permute-start(bf16[160,256]{1,0:T(8,128)(2,1)S(1)} %get-tuple-element.186), channel_id=1, source_target_pairs={{0,8},{4,12},{8,0},{12,4},{16,24},{20,28},{24,16},{28,20},{1,9},{5... | collective-permute-start | bytes 245768 | tf_op jit(solution)/shard_map/ppermute | solution.py:417
  111.8 12.1 %collective-permute-start.27 = (bf16[160,256]{1,0:T(8,128)(2,1)S(1)}, bf16[160,256]{1,0:T(8,128)(2,1)S(1)}, u32[]{:S(2)}, u32[]{:S(2)}) collective-permute-start(bf16[160,256]{1,0:T(8,128)(2,1)S(1)} %get-tuple-element.187), channel_id=1, source_target_pairs={{0,12},{4,8},{8,4},{12,0},{16,28},{20,24},{24,20},{28,16},{1,13},{... | collective-permute-start | bytes 245768 | tf_op jit(solution)/shard_map/ppermute | solution.py:417
  113.0 13.4 %collective-permute-start.28 = (bf16[160,256]{1,0:T(8,128)(2,1)S(1)}, bf16[160,256]{1,0:T(8,128)(2,1)S(1)}, u32[]{:S(2)}, u32[]{:S(2)}) collective-permute-start(bf16[160,256]{1,0:T(8,128)(2,1)S(1)} %get-tuple-element.188), channel_id=1, source_target_pairs={{0,16},{4,20},{8,24},{12,28},{16,0},{20,4},{24,8},{28,12},{1,17},{... | collective-permute-start | bytes 245768 | tf_op jit(solution)/shard_map/ppermute | solution.py:417
  116.4 10.8 %collective-permute-start.29 = (bf16[160,256]{1,0:T(8,128)(2,1)}, bf16[160,256]{1,0:T(8,128)(2,1)}, u32[]{:S(2)}, u32[]{:S(2)}) collective-permute-start(bf16[160,256]{1,0:T(8,128)(2,1)} %get-tuple-element.189), channel_id=1, source_target_pairs={{0,20},{4,16},{8,28},{12,24},{16,4},{20,0},{24,12},{28,8},{1,21},{... | collective-permute-start | bytes 245768 | tf_op jit(solution)/shard_map/ppermute | solution.py:417
  124.5 47.1 %collective-permute-start.14 = (bf16[128,2048]{1,0:T(8,128)(2,1)}, bf16[128,2048]{1,0:T(8,128)(2,1)S(1)}, u32[]{:S(2)}, u32[]{:S(2)}) collective-permute-start(bf16[128,2048]{1,0:T(8,128)(2,1)} %copy-done.94), channel_id=1, source_target_pairs={{0,4},{4,0},{8,12},{12,8},{16,20},{20,16},{24,28},{28,24},{1,5},{5... | collective-permute-start | bytes 1572872 | tf_op jit(solution)/shard_map/ppermute | solution.py:417
  127.0 44.7 %collective-permute-start.15 = (bf16[128,2048]{1,0:T(8,128)(2,1)}, bf16[128,2048]{1,0:T(8,128)(2,1)S(1)}, u32[]{:S(2)}, u32[]{:S(2)}) collective-permute-start(bf16[128,2048]{1,0:T(8,128)(2,1)} %copy-done.95), channel_id=1, source_target_pairs={{0,4},{4,0},{8,12},{12,8},{16,20},{20,16},{24,28},{28,24},{1,5},{5... | collective-permute-start | bytes 1572872 | tf_op jit(solution)/shard_map/ppermute | solution.py:417
  127.2 22.7 %collective-permute-start.17 = (f32[8,256]{1,0:T(8,128)S(1)}, f32[8,256]{1,0:T(8,128)S(1)}, u32[]{:S(2)}, u32[]{:S(2)}) collective-permute-start(f32[8,256]{1,0:T(8,128)S(1)} %slice.78), channel_id=1, source_target_pairs={{4,0},{8,4},{12,8},{16,12},{20,16},{24,20},{28,24},{5,1},{9,5},{13... | collective-permute-start | bytes 24584 | tf_op jit(solution)/shard_map/ppermute | solution.py:619
  132.1 21.3 %collective-permute-start.32 = (bf16[128,256]{1,0:T(8,128)(2,1)}, bf16[128,256]{1,0:T(8,128)(2,1)S(1)}, u32[]{:S(2)}, u32[]{:S(2)}) collective-permute-start(bf16[128,256]{1,0:T(8,128)(2,1)} %get-tuple-element.192.refs_0_), channel_id=1, source_target_pairs={{0,4},{4,0},{8,12},{12,8},{16,20},{20,16},{24,28},{28,24},{1,5},{5... | collective-permute-start | bytes 196616 | tf_op jit(solution)/shard_map/ppermute | solution.py:417
  157.5 12.3 %collective-permute-start.36 = (bf16[128,256]{1,0:T(8,128)(2,1)}, bf16[128,256]{1,0:T(8,128)(2,1)S(1)}, u32[]{:S(2)}, u32[]{:S(2)}) collective-permute-start(bf16[128,256]{1,0:T(8,128)(2,1)} %get-tuple-element.192.refs_0_), channel_id=1, source_target_pairs={{0,20},{4,16},{8,28},{12,24},{16,4},{20,0},{24,12},{28,8},{1,21},{... | collective-permute-start | bytes 196616 | tf_op jit(solution)/shard_map/ppermute | solution.py:417
  158.3 11.4 %collective-permute-start.37 = (bf16[128,256]{1,0:T(8,128)(2,1)}, bf16[128,256]{1,0:T(8,128)(2,1)S(1)}, u32[]{:S(2)}, u32[]{:S(2)}) collective-permute-start(bf16[128,256]{1,0:T(8,128)(2,1)} %get-tuple-element.192.refs_0_), channel_id=1, source_target_pairs={{0,24},{4,28},{8,16},{12,20},{16,8},{20,12},{24,0},{28,4},{1,25},{... | collective-permute-start | bytes 196616 | tf_op jit(solution)/shard_map/ppermute | solution.py:417
  (116 other events, 912.6 us)
